TPU v7x, 512 devices: a whole 4x8x8 slice. The times are simulated.
512 devices in a mesh: bias: 8 (over z_lo, x), gx: 8 (over z_hi, core), gy: 8 (over y).
Axes of the slice: x: 4, y: 8, z: 8 (z_hi: 4, z_lo: 2; z = z_hi * 2 + z_lo), core: 2. Of those that a mesh axis runs over, the one named last changes fastest.
Arguments:
- source: bfloat16 [8, 16, 24, 32, 256], P('bias', 'gx', 'gy'), may hold values from -6 to 6
- inverse: bfloat16 [8, 16, 24, 256, 256], P('bias', 'gx', 'gy'), may hold values from -0.375 to 0.375
- coupling: bfloat16 [8, 16, 24, 4, 256, 256], P('bias', 'gx', 'gy'), may hold values from -0.1875 to 0.1875
- sensitivity: float32 [8, 16, 24, 256], P('bias', 'gx', 'gy'), may hold values from -6 to 6
Outputs:
- adjoint_out: bfloat16 [8, 16, 24, 32, 256], P('bias', 'gx', 'gy')
- doping_grad: float32 [16, 24, 2048], P('gx', 'gy', 'bias')
All inputs are finite; a program needn't handle non-finite values.
Results may differ from a plain program's by a relative error of at most 0.02.
Values may be sent and summed in bfloat16 or wider, within the bound.
A program may use at most 64 MiB of HBM per device.

v0:
```python
import jax
import jax.numpy as jnp
from jax import lax
from jax.sharding import PartitionSpec as P

VARS = 4
ITERS = 3


def shifted(block, axis, distance):
    devices = range(lax.axis_size(axis))
    route = [(i - distance, i) for i in devices if i - distance in devices]
    return lax.ppermute(block, axis, route)


def shards(source, inverse, coupling, sensitivity):
    source_b = source[0]
    inverse_b = inverse[0]
    coupling_b = coupling[0]
    source_f = source_b.astype(jnp.float32)
    adjoint = jnp.einsum(
        "xyru,xyuv->xyrv", source_b, inverse_b, preferred_element_type=jnp.float32
    ).astype(jnp.bfloat16)
    for step in range(ITERS):
        products = jnp.einsum(
            "xyru,xyduv->xydrv", adjoint, coupling_b, preferred_element_type=jnp.float32
        ).astype(jnp.bfloat16)
        west_part = shifted(products[-1:, :, 0], "gx", 1)
        east_part = shifted(products[:1, :, 1], "gx", -1)
        south_part = shifted(products[:, -1:, 2], "gy", 1)
        north_part = shifted(products[:, :1, 3], "gy", -1)
        plus_x = jnp.concatenate([west_part, products[:-1, :, 0]], axis=0)
        minus_x = jnp.concatenate([products[1:, :, 1], east_part], axis=0)
        plus_y = jnp.concatenate([south_part, products[:, :-1, 2]], axis=1)
        minus_y = jnp.concatenate([products[:, 1:, 3], north_part], axis=1)
        incoming = (
            plus_x.astype(jnp.float32)
            + minus_x.astype(jnp.float32)
            + plus_y.astype(jnp.float32)
            + minus_y.astype(jnp.float32)
        )
        update = (source_f - incoming).astype(jnp.bfloat16)
        adjoint = jnp.einsum(
            "xyru,xyuv->xyrv", update, inverse_b, preferred_element_type=jnp.float32
        ).astype(jnp.bfloat16)
    blocks_x = adjoint.shape[0]
    blocks_y = adjoint.shape[1]
    sides = adjoint.shape[2]
    width = adjoint.shape[3] // VARS
    shaped = adjoint.astype(jnp.float32).reshape(blocks_x, blocks_y, sides, VARS, width)
    weights = sensitivity[0].reshape(blocks_x, blocks_y, 1, VARS, width)
    terms = jnp.sum(shaped * weights, axis=3).reshape(blocks_x, blocks_y, sides * width)
    summed = lax.psum(terms.astype(jnp.bfloat16), "bias").astype(jnp.float32)
    share = summed.shape[2] // lax.axis_size("bias")
    doping_grad = lax.dynamic_slice_in_dim(summed, lax.axis_index("bias") * share, share, 2)
    return (adjoint[None], doping_grad)


def solution(mesh):
    placed = (
        P("bias", "gx", "gy", None, None),
        P("bias", "gx", "gy", None, None),
        P("bias", "gx", "gy", None, None, None),
        P("bias", "gx", "gy", None),
    )
    return jax.shard_map(
        shards,
        mesh=mesh,
        in_specs=placed,
        out_specs=(P("bias", "gx", "gy", None, None), P("gx", "gy", "bias")),
        check_vma=False,
    )
```

profile of v0, /device:TPU:272, one launch (start us, length us, event | category | flops | bytes accessed | tf_op | source)
XLA Modules:
  0.0 102.6 jit_solution(6495505845985194345)
XLA Ops:
  0.6 1.9 %copy-done = bf16[1,2,3,4,256,256]{5,4,3,2,1,0:T(8,128)(2,1)S(1)} copy-done((bf16[1,2,3,4,256,256]{5,4,3,2,1,0:T(8,128)(2,1)S(1)}, bf16[1,2,3,4,256,256]{5,4,3,2,1,0:T(8,128)(2,1)}, u32[]{:S(2)}) %copy-start) | copy-done | bytes 3145752
  2.5 2.0 %fusion.10 = bf16[2,3,4,32,256]{4,3,2,1,0:T(8,128)(2,1)S(1)} fusion(bf16[1,2,3,256,256]{4,3,2,1,0:T(8,128)(2,1)} %param.5, bf16[1,2,3,32,256]{4,3,2,1,0:T(8,128)(2,1)} %param.4, bf16[1,2,3,4,256,256]{5,4,3,2,1,0:T(8,128)(2,1)S(1)} %copy-done), kind=kOutput, calls=%fused_computation.7 | convolution fusion | flops 126074880 | bytes 4423680 | tf_op jit(solution)/shard_map/xyru,xyduv->xydrv/dot_general | solution.py:25
  5.2 1.9 %collective-permute-start = (bf16[1,3,32,256]{3,2,1,0:T(8,128)(2,1)}, bf16[1,3,32,256]{3,2,1,0:T(8,128)(2,1)}, u32[]{:S(2)}, u32[]{:S(2)}) collective-permute-start(bf16[1,3,32,256]{3,2,1,0:T(8,128)(2,1)} %get-tuple-element.24), channel_id=1, source_target_pairs={{0,8},{8,16},{16,24},{24,32},{32,40},{40,48},{48,56},{1,9},{9,17},... | collective-permute-start | bytes 147464 | tf_op jit(solution)/shard_map/ppermute | solution.py:13
  7.1 5.8 %collective-permute-start.1 = (bf16[1,3,32,256]{3,2,1,0:T(8,128)(2,1)}, bf16[1,3,32,256]{3,2,1,0:T(8,128)(2,1)}, u32[]{:S(2)}, u32[]{:S(2)}) collective-permute-start(bf16[1,3,32,256]{3,2,1,0:T(8,128)(2,1)} %get-tuple-element.25), channel_id=1, source_target_pairs={{8,0},{16,8},{24,16},{32,24},{40,32},{48,40},{56,48},{9,1},{17,9},... | collective-permute-start | bytes 147464 | tf_op jit(solution)/shard_map/ppermute | solution.py:13
  13.5 2.3 %collective-permute-start.3 = (bf16[2,1,32,256]{3,2,0,1:T(8,128)(2,1)}, bf16[2,1,32,256]{3,2,0,1:T(8,128)(2,1)}, u32[]{:S(2)}, u32[]{:S(2)}) collective-permute-start(bf16[2,1,32,256]{3,2,0,1:T(8,128)(2,1)} %get-tuple-element.20), channel_id=1, source_target_pairs={{1,0},{2,1},{3,2},{4,3},{5,4},{6,5},{7,6},{9,8},{10,9},{11,10},{12... | collective-permute-start | bytes 98312 | tf_op jit(solution)/shard_map/ppermute | solution.py:13
  15.9 3.5 %collective-permute-start.2 = (bf16[2,1,32,256]{3,2,1,0:T(8,128)(2,1)}, bf16[2,1,32,256]{3,2,1,0:T(8,128)(2,1)}, u32[]{:S(2)}, u32[]{:S(2)}) collective-permute-start(bf16[2,1,32,256]{3,2,1,0:T(8,128)(2,1)} %get-tuple-element.21), channel_id=1, source_target_pairs={{0,1},{1,2},{2,3},{3,4},{4,5},{5,6},{6,7},{8,9},{9,10},{10,11},{11... | collective-permute-start | bytes 98312 | tf_op jit(solution)/shard_map/ppermute | solution.py:13
  20.8 1.2 %collective-permute-done.2 = bf16[2,1,32,256]{3,2,1,0:T(8,128)(2,1)} collective-permute-done((bf16[2,1,32,256]{3,2,1,0:T(8,128)(2,1)}, bf16[2,1,32,256]{3,2,1,0:T(8,128)(2,1)}, u32[]{:S(2)}, u32[]{:S(2)}) %collective-permute-start.2) | collective-permute-done | bytes 32800 | tf_op jit(solution)/shard_map/ppermute | solution.py:13
  22.0 1.6 %fusion.18 = bf16[2,3,32,256,1]{3,2,1,0,4:T(8,128)(2,1)S(1)} fusion(bf16[1,2,3,256,256]{4,3,2,1,0:T(8,128)(2,1)} %param.5, bf16[1,3,32,256]{3,2,1,0:T(8,128)(2,1)} %get-tuple-element.23, bf16[1,3,32,256]{3,2,1,0:T(8,128)(2,1)} %collective-permute-done, bf16[1,3,32,256]{3,2,1,0:T(8,128)(2,1)} %collective-permute-done.1, ...), kind=kOutput, calls=%fused_computation.15 | convolution fusion | flops 25903104 | bytes 1376256 | tf_op jit(solution)/shard_map/xyru,xyuv->xyrv/dot_general | solution.py:43
  24.3 2.1 %collective-permute-start.4 = (bf16[1,3,32,256]{3,2,0,1:T(8,128)(2,1)S(1)}, bf16[1,3,32,256]{3,2,0,1:T(8,128)(2,1)S(1)}, u32[]{:S(2)}, u32[]{:S(2)}) collective-permute-start(bf16[1,3,32,256]{3,2,0,1:T(8,128)(2,1)S(1)} %get-tuple-element.16), channel_id=1, source_target_pairs={{0,8},{8,16},{16,24},{24,32},{32,40},{40,48},{48,56},{1,9},{9,17},... | collective-permute-start | bytes 147464 | tf_op jit(solution)/shard_map/ppermute | solution.py:13
  26.4 5.8 %collective-permute-start.5 = (bf16[1,3,32,256]{3,2,0,1:T(8,128)(2,1)S(1)}, bf16[1,3,32,256]{3,2,0,1:T(8,128)(2,1)S(1)}, u32[]{:S(2)}, u32[]{:S(2)}) collective-permute-start(bf16[1,3,32,256]{3,2,0,1:T(8,128)(2,1)S(1)} %get-tuple-element.17), channel_id=1, source_target_pairs={{8,0},{16,8},{24,16},{32,24},{40,32},{48,40},{56,48},{9,1},{17,9},... | collective-permute-start | bytes 147464 | tf_op jit(solution)/shard_map/ppermute | solution.py:13
  32.2 4.0 %collective-permute-start.6 = (bf16[2,1,32,256]{3,2,0,1:T(8,128)(2,1)S(1)}, bf16[2,1,32,256]{3,2,0,1:T(8,128)(2,1)S(1)}, u32[]{:S(2)}, u32[]{:S(2)}) collective-permute-start(bf16[2,1,32,256]{3,2,0,1:T(8,128)(2,1)S(1)} %get-tuple-element.13), channel_id=1, source_target_pairs={{0,1},{1,2},{2,3},{3,4},{4,5},{5,6},{6,7},{8,9},{9,10},{10,11},{11... | collective-permute-start | bytes 98312 | tf_op jit(solution)/shard_map/ppermute | solution.py:13
  36.1 1.9 %collective-permute-start.7 = (bf16[2,1,32,256]{3,2,1,0:T(8,128)(2,1)S(1)}, bf16[2,1,32,256]{3,2,1,0:T(8,128)(2,1)S(1)}, u32[]{:S(2)}, u32[]{:S(2)}) collective-permute-start(bf16[2,1,32,256]{3,2,1,0:T(8,128)(2,1)S(1)} %get-tuple-element.12), channel_id=1, source_target_pairs={{1,0},{2,1},{3,2},{4,3},{5,4},{6,5},{7,6},{9,8},{10,9},{11,10},{12... | collective-permute-start | bytes 98312 | tf_op jit(solution)/shard_map/ppermute | solution.py:13
  38.1 5.4 %collective-permute-done.7 = bf16[2,1,32,256]{3,2,1,0:T(8,128)(2,1)S(1)} collective-permute-done((bf16[2,1,32,256]{3,2,1,0:T(8,128)(2,1)S(1)}, bf16[2,1,32,256]{3,2,1,0:T(8,128)(2,1)S(1)}, u32[]{:S(2)}, u32[]{:S(2)}) %collective-permute-start.7) | collective-permute-done | bytes 32800 | tf_op jit(solution)/shard_map/ppermute | solution.py:13
  43.5 1.1 %fusion.19 = bf16[2,3,32,256,1]{3,2,1,0,4:T(8,128)(2,1)S(1)} fusion(bf16[1,2,3,256,256]{4,3,2,1,0:T(8,128)(2,1)S(1)} %copy-done.1, bf16[2,1,32,256]{3,2,1,0:T(8,128)(2,1)S(1)} %collective-permute-done.7, bf16[1,2,3,32,256]{4,3,2,1,0:T(8,128)(2,1)} %param.4, bf16[1,3,32,256]{3,2,0,1:T(8,128)(2,1)S(1)} %get-tuple-element.15, ...), kind=kOutput, calls=%fused_computation.16 | convolution fusion | flops 26001408 | bytes 1376256 | tf_op jit(solution)/shard_map/xyru,xyuv->xyrv/dot_general | solution.py:43
  45.3 1.9 %collective-permute-start.8 = (bf16[1,3,32,256]{3,2,0,1:T(8,128)(2,1)S(1)}, bf16[1,3,32,256]{3,2,0,1:T(8,128)(2,1)S(1)}, u32[]{:S(2)}, u32[]{:S(2)}) collective-permute-start(bf16[1,3,32,256]{3,2,0,1:T(8,128)(2,1)S(1)} %get-tuple-element.8), channel_id=1, source_target_pairs={{0,8},{8,16},{16,24},{24,32},{32,40},{40,48},{48,56},{1,9},{9,17},... | collective-permute-start | bytes 147464 | tf_op jit(solution)/shard_map/ppermute | solution.py:13
  47.2 5.8 %collective-permute-start.9 = (bf16[1,3,32,256]{3,2,0,1:T(8,128)(2,1)S(1)}, bf16[1,3,32,256]{3,2,0,1:T(8,128)(2,1)S(1)}, u32[]{:S(2)}, u32[]{:S(2)}) collective-permute-start(bf16[1,3,32,256]{3,2,0,1:T(8,128)(2,1)S(1)} %get-tuple-element.9), channel_id=1, source_target_pairs={{8,0},{16,8},{24,16},{32,24},{40,32},{48,40},{56,48},{9,1},{17,9},... | collective-permute-start | bytes 147464 | tf_op jit(solution)/shard_map/ppermute | solution.py:13
  53.0 5.1 %collective-permute-start.10 = (bf16[2,1,32,256]{3,2,0,1:T(8,128)(2,1)S(1)}, bf16[2,1,32,256]{3,2,0,1:T(8,128)(2,1)S(1)}, u32[]{:S(2)}, u32[]{:S(2)}) collective-permute-start(bf16[2,1,32,256]{3,2,0,1:T(8,128)(2,1)S(1)} %get-tuple-element.5), channel_id=1, source_target_pairs={{0,1},{1,2},{2,3},{3,4},{4,5},{5,6},{6,7},{8,9},{9,10},{10,11},{11... | collective-permute-start | bytes 98312 | tf_op jit(solution)/shard_map/ppermute | solution.py:13
  58.1 1.9 %collective-permute-start.11 = (bf16[2,1,32,256]{3,2,1,0:T(8,128)(2,1)S(1)}, bf16[2,1,32,256]{3,2,1,0:T(8,128)(2,1)S(1)}, u32[]{:S(2)}, u32[]{:S(2)}) collective-permute-start(bf16[2,1,32,256]{3,2,1,0:T(8,128)(2,1)S(1)} %get-tuple-element.4), channel_id=1, source_target_pairs={{1,0},{2,1},{3,2},{4,3},{5,4},{6,5},{7,6},{9,8},{10,9},{11,10},{12... | collective-permute-start | bytes 98312 | tf_op jit(solution)/shard_map/ppermute | solution.py:13
  60.1 3.9 %collective-permute-done.11 = bf16[2,1,32,256]{3,2,1,0:T(8,128)(2,1)S(1)} collective-permute-done((bf16[2,1,32,256]{3,2,1,0:T(8,128)(2,1)S(1)}, bf16[2,1,32,256]{3,2,1,0:T(8,128)(2,1)S(1)}, u32[]{:S(2)}, u32[]{:S(2)}) %collective-permute-start.11) | collective-permute-done | bytes 32800 | tf_op jit(solution)/shard_map/ppermute | solution.py:13
  64.0 0.9 convolution_convert_fusion.1
  64.9 1.1 %reshape.16 = f32[2,3,32,4,64]{4,3,2,1,0:T(4,128)S(1)} reshape(bf16[2,3,32,256]{3,2,1,0:T(8,128)(2,1)} %convolution_convert_fusion.1) | data formatting | bytes 294912 | tf_op jit(solution)/shard_map/reshape | solution.py:50
  66.0 0.9 multiply_reduce_fusion
  66.9 0.9 reshape.20
  67.8 34.2 %psum.7 = bf16[2,3,2048]{2,0,1:T(2,128)(2,1)S(1)} all-reduce(bf16[2,3,2048]{2,0,1:T(2,128)(2,1)S(1)} %copy.80), channel_id=1, replica_groups=mesh['bias'=8,'gx'=8,'gy'=8] {'bias'}, use_global_device_ids=true, to_apply=%region_1.0 | all-reduce | flops 12288 | bytes 49152 | tf_op jit(solution)/shard_map/psum | solution.py:53
  (28 shorter events, 4.8 us)
Async XLA Ops:
  0.6 1.9 %copy-start = (bf16[1,2,3,4,256,256]{5,4,3,2,1,0:T(8,128)(2,1)S(1)}, bf16[1,2,3,4,256,256]{5,4,3,2,1,0:T(8,128)(2,1)}, u32[]{:S(2)}) copy-start(bf16[1,2,3,4,256,256]{5,4,3,2,1,0:T(8,128)(2,1)} %param.6) | copy-start | bytes 9437188
  5.2 16.8 %collective-permute-start = (bf16[1,3,32,256]{3,2,1,0:T(8,128)(2,1)}, bf16[1,3,32,256]{3,2,1,0:T(8,128)(2,1)}, u32[]{:S(2)}, u32[]{:S(2)}) collective-permute-start(bf16[1,3,32,256]{3,2,1,0:T(8,128)(2,1)} %get-tuple-element.24), channel_id=1, source_target_pairs={{0,8},{8,16},{16,24},{24,32},{32,40},{40,48},{48,56},{1,9},{9,17},... | collective-permute-start | bytes 147464 | tf_op jit(solution)/shard_map/ppermute | solution.py:13
  7.1 14.9 %collective-permute-start.1 = (bf16[1,3,32,256]{3,2,1,0:T(8,128)(2,1)}, bf16[1,3,32,256]{3,2,1,0:T(8,128)(2,1)}, u32[]{:S(2)}, u32[]{:S(2)}) collective-permute-start(bf16[1,3,32,256]{3,2,1,0:T(8,128)(2,1)} %get-tuple-element.25), channel_id=1, source_target_pairs={{8,0},{16,8},{24,16},{32,24},{40,32},{48,40},{56,48},{9,1},{17,9},... | collective-permute-start | bytes 147464 | tf_op jit(solution)/shard_map/ppermute | solution.py:13
  13.5 7.3 %collective-permute-start.3 = (bf16[2,1,32,256]{3,2,0,1:T(8,128)(2,1)}, bf16[2,1,32,256]{3,2,0,1:T(8,128)(2,1)}, u32[]{:S(2)}, u32[]{:S(2)}) collective-permute-start(bf16[2,1,32,256]{3,2,0,1:T(8,128)(2,1)} %get-tuple-element.20), channel_id=1, source_target_pairs={{1,0},{2,1},{3,2},{4,3},{5,4},{6,5},{7,6},{9,8},{10,9},{11,10},{12... | collective-permute-start | bytes 98312 | tf_op jit(solution)/shard_map/ppermute | solution.py:13
  15.9 6.1 %collective-permute-start.2 = (bf16[2,1,32,256]{3,2,1,0:T(8,128)(2,1)}, bf16[2,1,32,256]{3,2,1,0:T(8,128)(2,1)}, u32[]{:S(2)}, u32[]{:S(2)}) collective-permute-start(bf16[2,1,32,256]{3,2,1,0:T(8,128)(2,1)} %get-tuple-element.21), channel_id=1, source_target_pairs={{0,1},{1,2},{2,3},{3,4},{4,5},{5,6},{6,7},{8,9},{9,10},{10,11},{11... | collective-permute-start | bytes 98312 | tf_op jit(solution)/shard_map/ppermute | solution.py:13
  20.8 22.7 %copy-start.1 = (bf16[1,2,3,256,256]{4,3,2,1,0:T(8,128)(2,1)S(1)}, bf16[1,2,3,256,256]{4,3,2,1,0:T(8,128)(2,1)}, u32[]{:S(2)}) copy-start(bf16[1,2,3,256,256]{4,3,2,1,0:T(8,128)(2,1)} %param.5) | copy-start | bytes 2359300
  24.3 39.6 %copy-start.2 = (bf16[1,2,3,32,256]{4,3,2,1,0:T(8,128)(2,1)S(1)}, bf16[1,2,3,32,256]{4,3,2,1,0:T(8,128)(2,1)}, u32[]{:S(2)}) copy-start(bf16[1,2,3,32,256]{4,3,2,1,0:T(8,128)(2,1)} %param.4) | copy-start | bytes 294916
  24.3 19.1 %collective-permute-start.4 = (bf16[1,3,32,256]{3,2,0,1:T(8,128)(2,1)S(1)}, bf16[1,3,32,256]{3,2,0,1:T(8,128)(2,1)S(1)}, u32[]{:S(2)}, u32[]{:S(2)}) collective-permute-start(bf16[1,3,32,256]{3,2,0,1:T(8,128)(2,1)S(1)} %get-tuple-element.16), channel_id=1, source_target_pairs={{0,8},{8,16},{16,24},{24,32},{32,40},{40,48},{48,56},{1,9},{9,17},... | collective-permute-start | bytes 147464 | tf_op jit(solution)/shard_map/ppermute | solution.py:13
  26.4 17.0 %collective-permute-start.5 = (bf16[1,3,32,256]{3,2,0,1:T(8,128)(2,1)S(1)}, bf16[1,3,32,256]{3,2,0,1:T(8,128)(2,1)S(1)}, u32[]{:S(2)}, u32[]{:S(2)}) collective-permute-start(bf16[1,3,32,256]{3,2,0,1:T(8,128)(2,1)S(1)} %get-tuple-element.17), channel_id=1, source_target_pairs={{8,0},{16,8},{24,16},{32,24},{40,32},{48,40},{56,48},{9,1},{17,9},... | collective-permute-start | bytes 147464 | tf_op jit(solution)/shard_map/ppermute | solution.py:13
  32.2 5.9 %collective-permute-start.6 = (bf16[2,1,32,256]{3,2,0,1:T(8,128)(2,1)S(1)}, bf16[2,1,32,256]{3,2,0,1:T(8,128)(2,1)S(1)}, u32[]{:S(2)}, u32[]{:S(2)}) collective-permute-start(bf16[2,1,32,256]{3,2,0,1:T(8,128)(2,1)S(1)} %get-tuple-element.13), channel_id=1, source_target_pairs={{0,1},{1,2},{2,3},{3,4},{4,5},{5,6},{6,7},{8,9},{9,10},{10,11},{11... | collective-permute-start | bytes 98312 | tf_op jit(solution)/shard_map/ppermute | solution.py:13
  36.1 7.3 %collective-permute-start.7 = (bf16[2,1,32,256]{3,2,1,0:T(8,128)(2,1)S(1)}, bf16[2,1,32,256]{3,2,1,0:T(8,128)(2,1)S(1)}, u32[]{:S(2)}, u32[]{:S(2)}) collective-permute-start(bf16[2,1,32,256]{3,2,1,0:T(8,128)(2,1)S(1)} %get-tuple-element.12), channel_id=1, source_target_pairs={{1,0},{2,1},{3,2},{4,3},{5,4},{6,5},{7,6},{9,8},{10,9},{11,10},{12... | collective-permute-start | bytes 98312 | tf_op jit(solution)/shard_map/ppermute | solution.py:13
  45.3 18.6 %collective-permute-start.8 = (bf16[1,3,32,256]{3,2,0,1:T(8,128)(2,1)S(1)}, bf16[1,3,32,256]{3,2,0,1:T(8,128)(2,1)S(1)}, u32[]{:S(2)}, u32[]{:S(2)}) collective-permute-start(bf16[1,3,32,256]{3,2,0,1:T(8,128)(2,1)S(1)} %get-tuple-element.8), channel_id=1, source_target_pairs={{0,8},{8,16},{16,24},{24,32},{32,40},{40,48},{48,56},{1,9},{9,17},... | collective-permute-start | bytes 147464 | tf_op jit(solution)/shard_map/ppermute | solution.py:13
  47.2 16.7 %collective-permute-start.9 = (bf16[1,3,32,256]{3,2,0,1:T(8,128)(2,1)S(1)}, bf16[1,3,32,256]{3,2,0,1:T(8,128)(2,1)S(1)}, u32[]{:S(2)}, u32[]{:S(2)}) collective-permute-start(bf16[1,3,32,256]{3,2,0,1:T(8,128)(2,1)S(1)} %get-tuple-element.9), channel_id=1, source_target_pairs={{8,0},{16,8},{24,16},{32,24},{40,32},{48,40},{56,48},{9,1},{17,9},... | collective-permute-start | bytes 147464 | tf_op jit(solution)/shard_map/ppermute | solution.py:13
  53.0 7.1 %collective-permute-start.10 = (bf16[2,1,32,256]{3,2,0,1:T(8,128)(2,1)S(1)}, bf16[2,1,32,256]{3,2,0,1:T(8,128)(2,1)S(1)}, u32[]{:S(2)}, u32[]{:S(2)}) collective-permute-start(bf16[2,1,32,256]{3,2,0,1:T(8,128)(2,1)S(1)} %get-tuple-element.5), channel_id=1, source_target_pairs={{0,1},{1,2},{2,3},{3,4},{4,5},{5,6},{6,7},{8,9},{9,10},{10,11},{11... | collective-permute-start | bytes 98312 | tf_op jit(solution)/shard_map/ppermute | solution.py:13
  58.1 5.8 %collective-permute-start.11 = (bf16[2,1,32,256]{3,2,1,0:T(8,128)(2,1)S(1)}, bf16[2,1,32,256]{3,2,1,0:T(8,128)(2,1)S(1)}, u32[]{:S(2)}, u32[]{:S(2)}) collective-permute-start(bf16[2,1,32,256]{3,2,1,0:T(8,128)(2,1)S(1)} %get-tuple-element.4), channel_id=1, source_target_pairs={{1,0},{2,1},{3,2},{4,3},{5,4},{6,5},{7,6},{9,8},{10,9},{11,10},{12... | collective-permute-start | bytes 98312 | tf_op jit(solution)/shard_map/ppermute | solution.py:13
where the time goes:
time: 103 us
  starting transfers between devices  41.9 us (41%)
  blocking collectives  34.2 us (33%)
  waiting for transfers between devices  10.4 us (10%)
  matrix products  6.95 us (7%)
  local copies, waits for them, and re-layouts  6.77 us (7%)
  other arithmetic  1.53 us (1%)
    ppermute x12, starting transfers between devices, shifted(): return lax.ppermute(block, axis, route)  41.9 us
    psum x1, blocking collectives, shards(): summed = lax.psum(terms.astype(jnp.bfloat16), 'bias').astype(jnp.float32)  34.2 us
    ppermute x12, waiting for transfers between devices, shifted(): return lax.ppermute(block, axis, route)  10.4 us
    dot_general x3, matrix products, shards(): jnp.einsum('xyru,xyuv->xyrv', update, inverse_b, preferred_element_type=j...  3.69 us
    dot_general x3, matrix products, shards(): jnp.einsum('xyru,xyduv->xydrv', adjoint, coupling_b, preferred_element_ty...  3.26 us
  transfers between devices with their start and end apart: 12, of which 3 were waited for; matrix products, arithmetic and copies ran while one was open for 2% of the time, Pallas kernels for 0%

commit v1 on v0

v1 whole, which is shorter than its diff:
```python
import jax
import jax.numpy as jnp
from jax import lax
from jax.experimental import pallas as pl
from jax.experimental.pallas import tpu as pltpu
from jax.sharding import PartitionSpec as P

ITERS = 3
BX, BY = 2, 3
BLOCKS = BX * BY
RHS, UNK = 32, 256
PEERS = 8
MESH = pl.DeviceIdType.MESH


def mm(a, b):
    return jnp.dot(a, b, preferred_element_type=jnp.float32)


def kernel(src_h, inv_h, cp_h, sen_h, adj_out, dop_out,
           src, inv, cp, sen, xs, xr, ys, yr, gs, gr,
           lsem, isem, csem, xsend, xrecv, ysend, yrecv, gsend, grecv):
    bias, gx, gy = lax.axis_index("bias"), lax.axis_index("gx"), lax.axis_index("gy")
    nb, nx, ny = lax.axis_size("bias"), lax.axis_size("gx"), lax.axis_size("gy")
    xdev = (lax.rem(gx + nx - 1, nx), lax.rem(gx + 1, nx))
    ydev = (lax.rem(gy + ny - 1, ny), lax.rem(gy + 1, ny))

    barrier = pltpu.get_barrier_semaphore()
    for side in range(2):
        pl.semaphore_signal(barrier, inc=1, device_id={"gx": xdev[side]}, device_id_type=MESH)
        pl.semaphore_signal(barrier, inc=1, device_id={"gy": ydev[side]}, device_id_type=MESH)
    for step in range(1, PEERS):
        pl.semaphore_signal(barrier, inc=1, device_id={"bias": lax.rem(bias + step, nb)}, device_id_type=MESH)

    src_c = pltpu.make_async_copy(src_h, src, lsem.at[0])
    sen_c = pltpu.make_async_copy(sen_h, sen, lsem.at[1])
    src_c.start()
    inv_c = []
    for k in range(BLOCKS):
        c = pltpu.make_async_copy(inv_h.at[k], inv.at[k], isem.at[k])
        c.start()
        inv_c.append(c)
    first = [(j, 1) for j in range(BY)] + [(BY + j, 0) for j in range(BY)]
    first += [(0, 3), (BY, 3), (BY - 1, 2), (2 * BY - 1, 2)]
    rest = [(k, d) for k in range(BLOCKS) for d in range(4) if (k, d) not in first]
    cp_c = {}
    for k, d in first + rest:
        c = pltpu.make_async_copy(cp_h.at[k, d], cp.at[k, d], csem.at[k, d])
        c.start()
        cp_c[k, d] = c
    sen_c.start()

    has_x = (gx > 0, gx < nx - 1)
    has_y = (gy > 0, gy < ny - 1)

    src_c.wait()
    a = []
    for k in range(BLOCKS):
        inv_c[k].wait()
        a.append(mm(src[k], inv[k]).astype(jnp.bfloat16))

    sent = []
    for t in range(ITERS):
        if t == 0:
            for key in first:
                cp_c[key].wait()
        for j in range(BY):
            xs[t, 0, j] = mm(a[j], cp[j, 1]).astype(jnp.bfloat16)
            xs[t, 1, j] = mm(a[BY + j], cp[BY + j, 0]).astype(jnp.bfloat16)
        if t == 0:
            pl.semaphore_wait(barrier, 4 + PEERS - 1)
        for j in range(BY):
            for side in range(2):
                c = pltpu.make_async_remote_copy(
                    src_ref=xs.at[t, side, j], dst_ref=xr.at[t, 1 - side, j],
                    send_sem=xsend.at[t, side, j], recv_sem=xrecv.at[t, 1 - side, j],
                    device_id={"gx": xdev[side]}, device_id_type=MESH)
                c.start()
                sent.append(c)
        for i in range(BX):
            ys[t, 0, i] = mm(a[i * BY], cp[i * BY, 3]).astype(jnp.bfloat16)
            ys[t, 1, i] = mm(a[i * BY + BY - 1], cp[i * BY + BY - 1, 2]).astype(jnp.bfloat16)
        for i in range(BX):
            for side in range(2):
                c = pltpu.make_async_remote_copy(
                    src_ref=ys.at[t, side, i], dst_ref=yr.at[t, 1 - side, i],
                    send_sem=ysend.at[t, side, i], recv_sem=yrecv.at[t, 1 - side, i],
                    device_id={"gy": ydev[side]}, device_id_type=MESH)
                c.start()
                sent.append(c)
        if t == 0:
            for key in rest:
                cp_c[key].wait()
        acc = []
        for k in range(BLOCKS):
            i, j = divmod(k, BY)
            total = src[k].astype(jnp.float32)
            if i > 0:
                total = total - mm(a[k - BY], cp[k - BY, 0])
            if i < BX - 1:
                total = total - mm(a[k + BY], cp[k + BY, 1])
            if j > 0:
                total = total - mm(a[k - 1], cp[k - 1, 2])
            if j < BY - 1:
                total = total - mm(a[k + 1], cp[k + 1, 3])
            acc.append(total)
        for side in range(2):
            for i in range(BX):
                pltpu.make_async_copy(yr.at[t, side, i], yr.at[t, side, i], yrecv.at[t, side, i]).wait()
        for j in range(BY):
            for side in range(2):
                pltpu.make_async_copy(xr.at[t, side, j], xr.at[t, side, j], xrecv.at[t, side, j]).wait()
        new = []
        for k in range(BLOCKS):
            i, j = divmod(k, BY)
            total = acc[k]
            if i == 0:
                total = total - jnp.where(has_x[0], xr[t, 0, j].astype(jnp.float32), 0.0)
            if i == BX - 1:
                total = total - jnp.where(has_x[1], xr[t, 1, j].astype(jnp.float32), 0.0)
            if j == 0:
                total = total - jnp.where(has_y[0], yr[t, 0, i].astype(jnp.float32), 0.0)
            if j == BY - 1:
                total = total - jnp.where(has_y[1], yr[t, 1, i].astype(jnp.float32), 0.0)
            new.append(mm(total.astype(jnp.bfloat16), inv[k]).astype(jnp.bfloat16))
        a = new

    for k in range(BLOCKS):
        adj_out[k] = a[k]

    sen_c.wait()
    lane = lax.broadcasted_iota(jnp.int32, (RHS, 128), 1)
    staged = []
    for k in range(BLOCKS):
        i, j = divmod(k, BY)
        w = sen[j, pl.ds(i, 1), :]
        v = a[k].astype(jnp.float32) * w
        h = v[:, :128] + v[:, 128:]
        h = h + pltpu.roll(h, 64, 1)
        staged.append(jnp.where(lane < 64, h, pltpu.roll(h, RHS - 1, 0)).astype(jnp.bfloat16))
    rows = jnp.concatenate(staged, axis=0)
    r = lax.broadcasted_iota(jnp.int32, (PEERS * 16, BLOCKS * RHS), 0)
    c = lax.broadcasted_iota(jnp.int32, (PEERS * 16, BLOCKS * RHS), 1)
    place = lax.rem(r, 8)
    block = lax.rem(place, 2) * BY + lax.div(place, 2)
    wanted = jnp.where(place < BLOCKS, block * RHS + 2 * lax.div(r, 8), -1)
    pick = jnp.where(c == wanted, 1.0, 0.0).astype(jnp.bfloat16)
    gs[...] = mm(pick, rows).astype(jnp.bfloat16).reshape(PEERS, 16, 128)
    for step in range(1, PEERS):
        peer = lax.rem(bias + step, nb)
        c = pltpu.make_async_remote_copy(
            src_ref=gs.at[peer], dst_ref=gr.at[step], send_sem=gsend.at[step], recv_sem=grecv.at[step],
            device_id={"bias": peer}, device_id_type=MESH)
        c.start()
        sent.append(c)
    total = gs[bias].astype(jnp.float32)
    for step in range(1, PEERS):
        pltpu.make_async_copy(gr.at[step], gr.at[step], grecv.at[step]).wait()
        total = total + gr[step].astype(jnp.float32)
    for j in range(BY):
        dop_out[j, :, :128] = total[2 * j:2 * j + 2]
        dop_out[j, :, 128:] = total[8 + 2 * j:10 + 2 * j]
    for c in sent:
        c.wait_send()


def shards(source, inverse, coupling, sensitivity):
    src = source.reshape(BLOCKS, RHS, UNK)
    inv = inverse.reshape(BLOCKS, UNK, UNK)
    cp = coupling.reshape(BLOCKS, 4, UNK, UNK)
    sen = sensitivity.reshape(BX, BY, UNK).transpose(1, 0, 2)
    hbm = pl.BlockSpec(memory_space=pltpu.HBM)
    dma = pltpu.SemaphoreType.DMA
    adjoint, doping = pl.pallas_call(
        kernel,
        out_shape=(jax.ShapeDtypeStruct((BLOCKS, RHS, UNK), jnp.bfloat16),
                   jax.ShapeDtypeStruct((BY, BX, UNK), jnp.float32)),
        in_specs=[hbm] * 4,
        out_specs=(pl.BlockSpec(memory_space=pltpu.VMEM),) * 2,
        scratch_shapes=[
            pltpu.VMEM((BLOCKS, RHS, UNK), jnp.bfloat16),
            pltpu.VMEM((BLOCKS, UNK, UNK), jnp.bfloat16),
            pltpu.VMEM((BLOCKS, 4, UNK, UNK), jnp.bfloat16),
            pltpu.VMEM((BY, BX, UNK), jnp.float32),
            pltpu.VMEM((ITERS, 2, BY, RHS, UNK), jnp.bfloat16),
            pltpu.VMEM((ITERS, 2, BY, RHS, UNK), jnp.bfloat16),
            pltpu.VMEM((ITERS, 2, BX, RHS, UNK), jnp.bfloat16),
            pltpu.VMEM((ITERS, 2, BX, RHS, UNK), jnp.bfloat16),
            pltpu.VMEM((PEERS, 16, 128), jnp.bfloat16),
            pltpu.VMEM((PEERS, 16, 128), jnp.bfloat16),
            dma((2,)), dma((BLOCKS,)), dma((BLOCKS, 4)),
            dma((ITERS, 2, BY)), dma((ITERS, 2, BY)), dma((ITERS, 2, BX)), dma((ITERS, 2, BX)),
            dma((PEERS,)), dma((PEERS,)),
        ],
        compiler_params=pltpu.CompilerParams(
            collective_id=0, has_side_effects=True, vmem_limit_bytes=40 * 1024 * 1024),
        cost_estimate=pl.CostEstimate(flops=403_000_000, bytes_accessed=4_200_000, transcendentals=0),
    )(*(pltpu.with_memory_space_constraint(x, pltpu.HBM) for x in (src, inv, cp, sen)))
    return (adjoint.reshape(1, BX, BY, RHS, UNK), doping.transpose(1, 0, 2))


def solution(mesh):
    placed = (
        P("bias", "gx", "gy", None, None),
        P("bias", "gx", "gy", None, None),
        P("bias", "gx", "gy", None, None, None),
        P("bias", "gx", "gy", None),
    )
    return jax.shard_map(
        shards,
        mesh=mesh,
        in_specs=placed,
        out_specs=(P("bias", "gx", "gy", None, None), P("gx", "gy", "bias")),
        check_vma=False,
    )
```

time: 103 us -> 33.2 us (0.32)
  the two profiles are of different devices: /device:TPU:272 before, /device:TPU:16 now
where the time goes in v1:
time: 33.2 us; the launch traced here: 33.1 us
  Pallas kernels  31.2 us (94%)
  local copies, waits for them, and re-layouts  1.24 us (4%)
  between operations  0.64 us (2%)
    pallas_call x1, Pallas kernels, shards(): pl.pallas_call(kernel, out_shape=(jax.ShapeDtypeStruct((BLOCKS, RHS, UNK)...  31.2 us
    unnamed x2, local copies, waits for them, and re-layouts  1.24 us

profile of v1, /device:TPU:16, one launch (start us, length us, event | category | flops | bytes accessed | tf_op | source)
XLA Modules:
  0.0 33.1 jit_solution(6351612754252680626)
XLA Ops:
  0.6 31.2 %shard_map.59 = (bf16[6,32,256]{2,1,0:T(8,128)(2,1)S(1)}, f32[3,2,256]{2,1,0:T(2,128)S(1)}) custom-call(bf16[6,32,256]{2,1,0:T(8,128)(2,1)} %bitcast.12, bf16[6,256,256]{2,1,0:T(8,128)(2,1)} %bitcast.11, bf16[6,4,256,256]{3,2,1,0:T(8,128)(2,1)} %bitcast.10, f32[3,2,256]{2,1,0:T(2,128)} %bitcast.13), custom_call_target="tpu_custom_call" | custom-call | flops 403000000 | bytes 4200000 | tf_op jit(solution)/shard_map/pallas_call | solution.py:174
  31.8 0.6 %copy.8 = bf16[1,2,3,32,256]{4,3,2,1,0:T(8,128)(2,1)} copy(bf16[1,2,3,32,256]{4,3,2,1,0:T(8,128)(2,1)S(1)} %bitcast.8) | data formatting | bytes 196608
  32.5 0.6 %copy.9 = f32[2,3,256]{2,0,1:T(2,128)} copy(f32[2,3,256]{2,0,1:T(2,128)S(1)} %bitcast.9) | data formatting | bytes 12288

commit v2 on v1

v2 whole, which is shorter than its diff:
```python
import jax
import jax.numpy as jnp
from jax import lax
from jax.experimental import pallas as pl
from jax.experimental.pallas import tpu as pltpu
from jax.sharding import PartitionSpec as P

ITERS = 3
BX, BY = 2, 3
BLOCKS = BX * BY
RHS, UNK = 32, 256
PEERS = 8
MESH = pl.DeviceIdType.MESH


def mm(a, b):
    return jnp.dot(a, b, preferred_element_type=jnp.float32)


def whole(ref, sem):
    return pltpu.make_async_copy(ref, ref, sem)


def kernel(src_h, inv_h, cp_h, sen_h, adj_out, dop_out,
           src, inv, cp, sen, a, acc, zs, zr, cs, cr, ys, yr, gs, gr,
           lsem, ssem, zsem, csem, ysem, gsem):
    bias, gx, gy = lax.axis_index("bias"), lax.axis_index("gx"), lax.axis_index("gy")
    nb, nx, ny = lax.axis_size("bias"), lax.axis_size("gx"), lax.axis_size("gy")
    odd = lax.rem(gx, 2)
    far, near = odd * BY, (1 - odd) * BY
    zdev = {"gx": lax.rem(gx + nx + 2 * odd - 1, nx)}
    cdev = {"gx": gx + 1 - 2 * odd}
    ydev = ({"gy": lax.rem(gy + ny - 1, ny)}, {"gy": lax.rem(gy + 1, ny)})
    has_z = jnp.logical_and(gx + 2 * odd - 1 >= 0, gx + 2 * odd - 1 < nx)
    has_y = (gy > 0, gy < ny - 1)

    pltpu.make_async_copy(src_h, src, lsem.at[0]).start()
    pltpu.make_async_copy(inv_h, inv, lsem.at[1]).start()
    for j in range(BY):
        k = far + j
        pltpu.make_async_copy(cp_h.at[4 * k + 1 - odd], cp.at[4 * k + 1 - odd], lsem.at[2]).start()
    edge_y = [(i * BY + side * (BY - 1), 3 - side) for side in range(2) for i in range(BX)]
    for k, d in edge_y:
        pltpu.make_async_copy(cp_h.at[4 * k + d], cp.at[4 * k + d], lsem.at[3]).start()
    for j in range(BY):
        k = near + j
        pltpu.make_async_copy(cp_h.at[4 * k + odd], cp.at[4 * k + odd], lsem.at[4]).start()
    pltpu.make_async_copy(sen_h, sen, lsem.at[5]).start()

    barrier = pltpu.get_barrier_semaphore()
    for dev in (zdev, cdev) + ydev:
        pl.semaphore_signal(barrier, inc=1, device_id=dev, device_id_type=MESH)
    for step in range(1, PEERS):
        pl.semaphore_signal(barrier, inc=1, device_id={"bias": lax.rem(bias + step, nb)}, device_id_type=MESH)

    whole(src, lsem.at[0]).wait()
    whole(inv, lsem.at[1]).wait()
    inner = [(j, 0) for j in range(BY)] + [(BY + j, 1) for j in range(BY)]
    inner += [(i * BY + j, 2) for i in range(BX) for j in range(BY - 1)]
    inner += [(i * BY + j, 3) for i in range(BX) for j in range(1, BY)]
    for k, d in inner:
        pltpu.make_async_copy(cp_h.at[4 * k + d], cp.at[4 * k + d], lsem.at[6]).start()
    for k in range(BLOCKS):
        a[k] = mm(src[k], inv[k]).astype(jnp.bfloat16)

    for t in range(ITERS):
        if t == 0:
            whole(cp.at[pl.ds(0, BY)], lsem.at[2]).wait()
        for j in range(BY):
            zs[t, j] = mm(a[far + j], cp[4 * (far + j) + 1 - odd]).astype(jnp.bfloat16)
        if t == 0:
            pl.semaphore_wait(barrier, 4 + PEERS - 1)
        for j in range(BY):
            pltpu.make_async_remote_copy(
                src_ref=zs.at[t, j], dst_ref=zr.at[t, j], send_sem=ssem.at[0], recv_sem=zsem.at[t, j],
                device_id=zdev, device_id_type=MESH).start()
        if t == 0:
            whole(cp.at[pl.ds(0, 2 * BX)], lsem.at[3]).wait()
        for side in range(2):
            for i in range(BX):
                k, d = edge_y[side * BX + i]
                ys[t, side, i] = mm(a[k], cp[4 * k + d]).astype(jnp.bfloat16)
        for side in range(2):
            pltpu.make_async_remote_copy(
                src_ref=ys.at[t, side], dst_ref=yr.at[t, 1 - side], send_sem=ssem.at[1], recv_sem=ysem.at[t, 1 - side],
                device_id=ydev[side], device_id_type=MESH).start()
        if t == 0:
            whole(cp.at[pl.ds(0, BY)], lsem.at[4]).wait()
        for j in range(BY):
            cs[t, j] = mm(a[near + j], cp[4 * (near + j) + odd]).astype(jnp.bfloat16)
        pltpu.make_async_remote_copy(
            src_ref=cs.at[t], dst_ref=cr.at[t], send_sem=ssem.at[2], recv_sem=csem.at[t],
            device_id=cdev, device_id_type=MESH).start()
        if t == 0:
            whole(cp.at[pl.ds(0, len(inner))], lsem.at[6]).wait()
        for k in range(BLOCKS):
            i, j = divmod(k, BY)
            total = src[k].astype(jnp.float32)
            if i > 0:
                total = total - mm(a[k - BY], cp[4 * (k - BY)])
            if i < BX - 1:
                total = total - mm(a[k + BY], cp[4 * (k + BY) + 1])
            if j > 0:
                total = total - mm(a[k - 1], cp[4 * (k - 1) + 2])
            if j < BY - 1:
                total = total - mm(a[k + 1], cp[4 * (k + 1) + 3])
            acc[k] = total
        whole(cr.at[t], csem.at[t]).wait()
        near_u = [acc[near + j] - cr[t, j].astype(jnp.float32) for j in range(BY)]
        a[near + 1] = mm(near_u[1].astype(jnp.bfloat16), inv[near + 1]).astype(jnp.bfloat16)
        for side in range(2):
            whole(yr.at[t, side], ysem.at[t, side]).wait()
        for side in range(2):
            j = side * (BY - 1)
            u = near_u[j] - jnp.where(has_y[side], yr[t, side, 1 - odd].astype(jnp.float32), 0.0)
            a[near + j] = mm(u.astype(jnp.bfloat16), inv[near + j]).astype(jnp.bfloat16)
        far_u = [acc[far + j] for j in range(BY)]
        for side in range(2):
            j = side * (BY - 1)
            far_u[j] = far_u[j] - jnp.where(has_y[side], yr[t, side, odd].astype(jnp.float32), 0.0)
        for j in range(BY):
            whole(zr.at[t, j], zsem.at[t, j]).wait()
        for j in range(BY):
            u = far_u[j] - jnp.where(has_z, zr[t, j].astype(jnp.float32), 0.0)
            a[far + j] = mm(u.astype(jnp.bfloat16), inv[far + j]).astype(jnp.bfloat16)

    whole(sen, lsem.at[5]).wait()
    lane = lax.broadcasted_iota(jnp.int32, (RHS, 128), 1)
    staged = []
    for k in range(BLOCKS):
        i, j = divmod(k, BY)
        w = sen[j, pl.ds(i, 1), :]
        v = a[k].astype(jnp.float32) * w
        h = v[:, :128] + v[:, 128:]
        h = h + pltpu.roll(h, 64, 1)
        staged.append(jnp.where(lane < 64, h, pltpu.roll(h, RHS - 1, 0)).astype(jnp.bfloat16))
    rows = jnp.concatenate(staged, axis=0)
    r = lax.broadcasted_iota(jnp.int32, (PEERS * 16, BLOCKS * RHS), 0)
    c = lax.broadcasted_iota(jnp.int32, (PEERS * 16, BLOCKS * RHS), 1)
    place = lax.rem(r, 8)
    block = lax.rem(place, 2) * BY + lax.div(place, 2)
    wanted = jnp.where(place < BLOCKS, block * RHS + 2 * lax.div(r, 8), -1)
    pick = jnp.where(c == wanted, 1.0, 0.0).astype(jnp.bfloat16)
    gs[...] = mm(pick, rows).astype(jnp.bfloat16).reshape(PEERS, 16, 128)
    for step in (6, 2, 5, 7, 1, 3, 4):
        peer = lax.rem(bias + step, nb)
        pltpu.make_async_remote_copy(
            src_ref=gs.at[peer], dst_ref=gr.at[step - 1], send_sem=ssem.at[3], recv_sem=gsem,
            device_id={"bias": peer}, device_id_type=MESH).start()
    adj_out[...] = a[...]
    total = gs[bias].astype(jnp.float32)
    whole(gr, gsem).wait()
    for step in range(1, PEERS):
        total = total + gr[step - 1].astype(jnp.float32)
    for j in range(BY):
        dop_out[j, :, :128] = total[2 * j:2 * j + 2]
        dop_out[j, :, 128:] = total[8 + 2 * j:10 + 2 * j]
    whole(zs, ssem.at[0]).wait()
    whole(ys, ssem.at[1]).wait()
    whole(cs, ssem.at[2]).wait()
    whole(gs.at[pl.ds(0, PEERS - 1)], ssem.at[3]).wait()


def shards(source, inverse, coupling, sensitivity):
    src = source.reshape(BLOCKS, RHS, UNK)
    inv = inverse.reshape(BLOCKS, UNK, UNK)
    cp = coupling.reshape(BLOCKS * 4, UNK, UNK)
    sen = sensitivity.reshape(BX, BY, UNK).transpose(1, 0, 2)
    hbm = pl.BlockSpec(memory_space=pltpu.HBM)
    dma = pltpu.SemaphoreType.DMA
    adjoint, doping = pl.pallas_call(
        kernel,
        out_shape=(jax.ShapeDtypeStruct((BLOCKS, RHS, UNK), jnp.bfloat16),
                   jax.ShapeDtypeStruct((BY, BX, UNK), jnp.float32)),
        in_specs=[hbm] * 4,
        out_specs=(pl.BlockSpec(memory_space=pltpu.VMEM),) * 2,
        scratch_shapes=[
            pltpu.VMEM((BLOCKS, RHS, UNK), jnp.bfloat16),
            pltpu.VMEM((BLOCKS, UNK, UNK), jnp.bfloat16),
            pltpu.VMEM((BLOCKS * 4, UNK, UNK), jnp.bfloat16),
            pltpu.VMEM((BY, BX, UNK), jnp.float32),
            pltpu.VMEM((BLOCKS, RHS, UNK), jnp.bfloat16),
            pltpu.VMEM((BLOCKS, RHS, UNK), jnp.float32),
            pltpu.VMEM((ITERS, BY, RHS, UNK), jnp.bfloat16),
            pltpu.VMEM((ITERS, BY, RHS, UNK), jnp.bfloat16),
            pltpu.VMEM((ITERS, BY, RHS, UNK), jnp.bfloat16),
            pltpu.VMEM((ITERS, BY, RHS, UNK), jnp.bfloat16),
            pltpu.VMEM((ITERS, 2, BX, RHS, UNK), jnp.bfloat16),
            pltpu.VMEM((ITERS, 2, BX, RHS, UNK), jnp.bfloat16),
            pltpu.VMEM((PEERS, 16, 128), jnp.bfloat16),
            pltpu.VMEM((PEERS - 1, 16, 128), jnp.bfloat16),
            dma((7,)), dma((4,)), dma((ITERS, BY)), dma((ITERS,)), dma((ITERS, 2)), dma(()),
        ],
        compiler_params=pltpu.CompilerParams(
            collective_id=0, has_side_effects=True, vmem_limit_bytes=40 * 1024 * 1024),
        cost_estimate=pl.CostEstimate(flops=403_000_000, bytes_accessed=4_200_000, transcendentals=0),
    )(*(pltpu.with_memory_space_constraint(x, pltpu.HBM) for x in (src, inv, cp, sen)))
    return (adjoint.reshape(1, BX, BY, RHS, UNK), doping.transpose(1, 0, 2))


def solution(mesh):
    placed = (
        P("bias", "gx", "gy", None, None),
        P("bias", "gx", "gy", None, None),
        P("bias", "gx", "gy", None, None, None),
        P("bias", "gx", "gy", None),
    )
    return jax.shard_map(
        shards,
        mesh=mesh,
        in_specs=placed,
        out_specs=(P("bias", "gx", "gy", None, None), P("gx", "gy", "bias")),
        check_vma=False,
    )
```

time: 33.2 us -> 31.2 us (0.940)
  the two profiles are of different devices: /device:TPU:16 before, /device:TPU:24 now
where the time goes in v2:
time: 31.2 us; the launch traced here: 31 us
  Pallas kernels  29.2 us (94%)
  local copies, waits for them, and re-layouts  1.24 us (4%)
  between operations  0.64 us (2%)
    pallas_call x1, Pallas kernels, shards(): pl.pallas_call(kernel, out_shape=(jax.ShapeDtypeStruct((BLOCKS, RHS, UNK)...  29.2 us
    unnamed x2, local copies, waits for them, and re-layouts  1.24 us

profile of v2, /device:TPU:24, one launch (start us, length us, event | category | flops | bytes accessed | tf_op | source)
XLA Modules:
  0.0 31.0 jit_solution(280225688264760997)
XLA Ops:
  0.6 29.2 %shard_map.59 = (bf16[6,32,256]{2,1,0:T(8,128)(2,1)S(1)}, f32[3,2,256]{2,1,0:T(2,128)S(1)}) custom-call(bf16[6,32,256]{2,1,0:T(8,128)(2,1)} %bitcast.12, bf16[6,256,256]{2,1,0:T(8,128)(2,1)} %bitcast.11, bf16[24,256,256]{2,1,0:T(8,128)(2,1)} %bitcast.10, f32[3,2,256]{2,1,0:T(2,128)} %bitcast.13), custom_call_target="tpu_custom_call" | custom-call | flops 403000000 | bytes 4200000 | tf_op jit(solution)/shard_map/pallas_call | solution.py:171
  29.8 0.6 %copy.8 = bf16[1,2,3,32,256]{4,3,2,1,0:T(8,128)(2,1)} copy(bf16[1,2,3,32,256]{4,3,2,1,0:T(8,128)(2,1)S(1)} %bitcast.8) | data formatting | bytes 196608
  30.4 0.6 %copy.9 = f32[2,3,256]{2,0,1:T(2,128)} copy(f32[2,3,256]{2,0,1:T(2,128)S(1)} %bitcast.9) | data formatting | bytes 12288

commit v3 on v2

v3 whole, which is shorter than its diff:
```python
import jax
import jax.numpy as jnp
from jax import lax
from jax.experimental import pallas as pl
from jax.experimental.pallas import tpu as pltpu
from jax.sharding import PartitionSpec as P

ITERS = 3
BX, BY = 2, 3
BLOCKS = BX * BY
RHS, UNK = 32, 256
PEERS = 8
MESH = pl.DeviceIdType.MESH


def mm(a, b):
    return jnp.dot(a, b, preferred_element_type=jnp.float32)


def whole(ref, sem):
    return pltpu.make_async_copy(ref, ref, sem)


def kernel(src_h, inv_h, cp_h, sen_h, adj_out, dop_out,
           src, inv, cp, sen, a, acc, zs, zr, cs, cr, ys, yr, fold, wz, wy, wr, gs, gr,
           lsem, ssem, zsem, csem, ysem, wsem, gsem):
    bias, gx, gy = lax.axis_index("bias"), lax.axis_index("gx"), lax.axis_index("gy")
    nb, nx, ny = lax.axis_size("bias"), lax.axis_size("gx"), lax.axis_size("gy")
    odd = lax.rem(gx, 2)
    far, near = odd * BY, (1 - odd) * BY
    zdev = {"gx": lax.rem(gx + nx + 2 * odd - 1, nx)}
    cdev = {"gx": gx + 1 - 2 * odd}
    ydev = ({"gy": lax.rem(gy + ny - 1, ny)}, {"gy": lax.rem(gy + 1, ny)})
    has_z = jnp.logical_and(gx + 2 * odd - 1 >= 0, gx + 2 * odd - 1 < nx)
    has_y = (gy > 0, gy < ny - 1)
    peers = [lax.rem(bias + step, nb) for step in range(PEERS)]

    def load(from_ref, to_ref, sem):
        pltpu.make_async_copy(from_ref, to_ref, lsem.at[sem]).start()

    def load_tile(k, sem):
        load(cp_h.at[k], cp.at[k], sem)

    def product(k, d):
        return mm(a[k], cp[4 * k + d]).astype(jnp.bfloat16)

    def send(from_ref, to_ref, sent, landed, dev):
        pltpu.make_async_remote_copy(
            src_ref=from_ref, dst_ref=to_ref, send_sem=ssem.at[sent], recv_sem=landed,
            device_id=dev, device_id_type=MESH).start()

    far_rows, near_rows = pl.ds(far, BY), pl.ds(near, BY)
    load(src_h, src, 0)
    load(inv_h.at[far_rows], inv.at[far_rows], 1)
    barrier = pltpu.get_barrier_semaphore()
    for dev in (zdev,) + ydev + (cdev,):
        pl.semaphore_signal(barrier, inc=1, device_id=dev, device_id_type=MESH)
    for j in range(BY):
        load_tile(4 * (far + j) + 1 - odd, 2)
    for peer in peers[1:]:
        pl.semaphore_signal(barrier, inc=1, device_id={"bias": peer}, device_id_type=MESH)
    load(inv_h.at[near_rows], inv.at[near_rows], 3)
    edge_y = [(i * BY + side * (BY - 1), 3 - side) for side in range(2) for i in range(BX)]
    for k, d in edge_y:
        load_tile(4 * k + d, 4)
    for j in range(BY):
        load_tile(4 * (near + j) + odd, 5)
    load(sen_h, sen, 6)

    whole(src, lsem.at[0]).wait()
    whole(inv.at[far_rows], lsem.at[1]).wait()
    for j in range(BY):
        a[far + j] = mm(src[far + j], inv[far + j]).astype(jnp.bfloat16)
    inner = [(j, 0) for j in range(BY)] + [(BY + j, 1) for j in range(BY)]
    inner += [(i * BY + j, 2) for i in range(BX) for j in range(BY - 1)]
    inner += [(i * BY + j, 3) for i in range(BX) for j in range(1, BY)]
    lane_w = lax.broadcasted_iota(jnp.int32, (UNK, 128), 1) < 64
    lane_e = lax.broadcasted_iota(jnp.int32, (RHS, 128), 1) < 64
    lane_g = lax.broadcasted_iota(jnp.int32, (4, 128), 1) < 64

    for t in range(ITERS):
        if t == 0:
            whole(cp.at[pl.ds(0, BY)], lsem.at[2]).wait()
        for j in range(BY):
            zs[t, j] = product(far + j, 1 - odd)
        if t == 0:
            pl.semaphore_wait(barrier, 3 + PEERS)
        for j in range(BY):
            send(zs.at[t, j], zr.at[t, j], 0, zsem.at[t, j], zdev)
        if t == 0:
            for k, d in inner:
                load_tile(4 * k + d, 7)
            whole(inv.at[near_rows], lsem.at[3]).wait()
            for j in range(BY):
                a[near + j] = mm(src[near + j], inv[near + j]).astype(jnp.bfloat16)
            whole(cp.at[pl.ds(0, 2 * BX)], lsem.at[4]).wait()
        for side in range(2):
            for i in range(BX):
                k, d = edge_y[side * BX + i]
                ys[t, side, i] = product(k, d)
        for side in range(2):
            send(ys.at[t, side], yr.at[t, 1 - side], 1, ysem.at[t, 1 - side], ydev[side])
        if t == 0:
            whole(cp.at[pl.ds(0, BY)], lsem.at[5]).wait()
        for j in range(BY):
            cs[t, j] = product(near + j, odd)
        send(cs.at[t], cr.at[t], 2, csem.at[t], cdev)
        if t == ITERS - 1:
            whole(wr, wsem).wait()
            parts = [jnp.where(lane_e, mm(zs[t, 0], wr[0]), mm(zs[t, 1], wr[0])), mm(zs[t, 2], wr[1])]
            for m, part in enumerate(parts):
                for p in range(PEERS):
                    gs[p, m] = part[4 * p:4 * p + 4]
            for step in range(PEERS - 1, -1, -1):
                send(gs.at[peers[step], pl.ds(0, 2)], gr.at[pl.ds(2 * step, 2)], 3, gsem, {"bias": peers[step], **zdev})
            for side in range(2):
                part = jnp.where(lane_e, mm(ys[t, side, 0], wr[2 + side]), mm(ys[t, side, 1], wr[2 + side]))
                for p in range(PEERS):
                    gs[p, 2 + side] = part[4 * p:4 * p + 4]
            for side in range(2):
                for step in range(PEERS - 1, -1, -1):
                    send(gs.at[peers[step], pl.ds(2 + side, 1)], gr.at[pl.ds(16 + 8 * (1 - side) + step, 1)], 3, gsem,
                         {"bias": peers[step], **ydev[side]})
        if t == 0:
            whole(cp.at[pl.ds(0, len(inner))], lsem.at[7]).wait()
        for k in range(BLOCKS):
            i, j = divmod(k, BY)
            total = src[k].astype(jnp.float32)
            if i > 0:
                total = total - mm(a[k - BY], cp[4 * (k - BY)])
            if i < BX - 1:
                total = total - mm(a[k + BY], cp[4 * (k + BY) + 1])
            if j > 0:
                total = total - mm(a[k - 1], cp[4 * (k - 1) + 2])
            if j < BY - 1:
                total = total - mm(a[k + 1], cp[4 * (k + 1) + 3])
            acc[k] = total
        if t == 0:
            whole(sen, lsem.at[6]).wait()
            for k in range(BLOCKS):
                i, j = divmod(k, BY)
                h = inv[k].astype(jnp.float32) * sen[j, i:i + 1, :]
                h = h[:, :128] + h[:, 128:]
                fold[k] = h + pltpu.roll(h, 64, 1)
            for j in range(BY):
                wy[j] = jnp.where(lane_w, fold[j], fold[BY + j]).astype(jnp.bfloat16)
            wz[0] = jnp.where(lane_w, fold[far], fold[far + 1]).astype(jnp.bfloat16)
            wz[1] = fold[far + 2].astype(jnp.bfloat16)
            for side in range(2):
                send(wy.at[side * (BY - 1)], wr.at[3 - side], 4, wsem, ydev[side])
        if t < ITERS - 1:
            send(wz.at[t], wr.at[t], 4, wsem, zdev)
        whole(cr.at[t], csem.at[t]).wait()
        for j in range(BY):
            acc[near + j] = acc[near + j] - cr[t, j].astype(jnp.float32)
        if t == ITERS - 1:
            for j in range(BY):
                part = jnp.where(lane_e, mm(acc[j].astype(jnp.bfloat16), wy[j]), mm(acc[BY + j].astype(jnp.bfloat16), wy[j]))
                for p in range(PEERS):
                    gs[p, 4 + j] = part[4 * p:4 * p + 4]
            for step in (6, 2, 5, 7, 1, 3, 4):
                send(gs.at[peers[step], pl.ds(4, 3)], gr.at[pl.ds(32 + 3 * (step - 1), 3)], 3, gsem, {"bias": peers[step]})
        near_u = [acc[near + j] for j in range(BY)]
        a[near + 1] = mm(near_u[1].astype(jnp.bfloat16), inv[near + 1]).astype(jnp.bfloat16)
        for side in range(2):
            whole(yr.at[t, side], ysem.at[t, side]).wait()
        for side in range(2):
            j = side * (BY - 1)
            u = near_u[j] - jnp.where(has_y[side], yr[t, side, 1 - odd].astype(jnp.float32), 0.0)
            a[near + j] = mm(u.astype(jnp.bfloat16), inv[near + j]).astype(jnp.bfloat16)
        far_u = [acc[far + j] for j in range(BY)]
        for side in range(2):
            j = side * (BY - 1)
            far_u[j] = far_u[j] - jnp.where(has_y[side], yr[t, side, odd].astype(jnp.float32), 0.0)
        for j in range(BY):
            whole(zr.at[t, j], zsem.at[t, j]).wait()
        for j in range(BY):
            u = far_u[j] - jnp.where(has_z, zr[t, j].astype(jnp.float32), 0.0)
            a[far + j] = mm(u.astype(jnp.bfloat16), inv[far + j]).astype(jnp.bfloat16)

    adj_out[...] = a[...]
    whole(zs, ssem.at[0]).wait()
    whole(ys, ssem.at[1]).wait()
    whole(cs, ssem.at[2]).wait()
    whole(wr, ssem.at[4]).wait()
    totals = [gs[bias, 4 + j] for j in range(BY)]
    whole(gr, gsem).wait()
    for step in range(1, PEERS):
        for j in range(BY):
            totals[j] = totals[j] + gr[32 + 3 * (step - 1) + j]
    for side in range(2):
        part = gr[16 + 8 * side]
        for step in range(1, PEERS):
            part = part + gr[16 + 8 * side + step]
        j = side * (BY - 1)
        totals[j] = totals[j] - jnp.where(has_y[side], part, 0.0)
    pair, last = gr[0], gr[1]
    for step in range(1, PEERS):
        pair, last = pair + gr[2 * step], last + gr[2 * step + 1]
    turned = pltpu.roll(pair, 64, 1)
    half = lax.broadcasted_iota(jnp.int32, (4, 128), 1) // 64 == jnp.where(has_z, odd, -1)
    for j, part in enumerate((jnp.where(lane_g, pair, turned), jnp.where(lane_g, turned, pair), last)):
        here = totals[j] - jnp.where(half, part, 0.0)
        other = pltpu.roll(here, 64, 1)
        for q in range(0, 4, 2):
            dop_out[j, 0:1, 64 * q:64 * q + 128] = jnp.where(lane_g[:1], here[q:q + 1], other[q + 1:q + 2])
            dop_out[j, 1:2, 64 * q:64 * q + 128] = jnp.where(lane_g[:1], other[q:q + 1], here[q + 1:q + 2])
    whole(gr, ssem.at[3]).wait()


def shards(source, inverse, coupling, sensitivity):
    src = source.reshape(BLOCKS, RHS, UNK)
    inv = inverse.reshape(BLOCKS, UNK, UNK)
    cp = coupling.reshape(BLOCKS * 4, UNK, UNK)
    sen = sensitivity.reshape(BX, BY, UNK).transpose(1, 0, 2)
    hbm = pl.BlockSpec(memory_space=pltpu.HBM)
    dma = pltpu.SemaphoreType.DMA
    adjoint, doping = pl.pallas_call(
        kernel,
        out_shape=(jax.ShapeDtypeStruct((BLOCKS, RHS, UNK), jnp.bfloat16),
                   jax.ShapeDtypeStruct((BY, BX, UNK), jnp.float32)),
        in_specs=[hbm] * 4,
        out_specs=(pl.BlockSpec(memory_space=pltpu.VMEM),) * 2,
        scratch_shapes=[
            pltpu.VMEM((BLOCKS, RHS, UNK), jnp.bfloat16),
            pltpu.VMEM((BLOCKS, UNK, UNK), jnp.bfloat16),
            pltpu.VMEM((BLOCKS * 4, UNK, UNK), jnp.bfloat16),
            pltpu.VMEM((BY, BX, UNK), jnp.float32),
            pltpu.VMEM((BLOCKS, RHS, UNK), jnp.bfloat16),
            pltpu.VMEM((BLOCKS, RHS, UNK), jnp.float32),
            pltpu.VMEM((ITERS, BY, RHS, UNK), jnp.bfloat16),
            pltpu.VMEM((ITERS, BY, RHS, UNK), jnp.bfloat16),
            pltpu.VMEM((ITERS, BY, RHS, UNK), jnp.bfloat16),
            pltpu.VMEM((ITERS, BY, RHS, UNK), jnp.bfloat16),
            pltpu.VMEM((ITERS, 2, BX, RHS, UNK), jnp.bfloat16),
            pltpu.VMEM((ITERS, 2, BX, RHS, UNK), jnp.bfloat16),
            pltpu.VMEM((BLOCKS, UNK, 128), jnp.float32),
            pltpu.VMEM((2, UNK, 128), jnp.bfloat16),
            pltpu.VMEM((BY, UNK, 128), jnp.bfloat16),
            pltpu.VMEM((4, UNK, 128), jnp.bfloat16),
            pltpu.VMEM((PEERS, 7, 4, 128), jnp.float32),
            pltpu.VMEM((16 + 16 + 3 * (PEERS - 1), 4, 128), jnp.float32),
            dma((8,)), dma((5,)), dma((ITERS, BY)), dma((ITERS,)), dma((ITERS, 2)), dma(()), dma(()),
        ],
        compiler_params=pltpu.CompilerParams(
            collective_id=0, has_side_effects=True, vmem_limit_bytes=40 * 1024 * 1024),
        cost_estimate=pl.CostEstimate(flops=403_000_000, bytes_accessed=4_200_000, transcendentals=0),
    )(*(pltpu.with_memory_space_constraint(x, pltpu.HBM) for x in (src, inv, cp, sen)))
    return (adjoint.reshape(1, BX, BY, RHS, UNK), doping.transpose(1, 0, 2))


def solution(mesh):
    placed = (
        P("bias", "gx", "gy", None, None),
        P("bias", "gx", "gy", None, None),
        P("bias", "gx", "gy", None, None, None),
        P("bias", "gx", "gy", None),
    )
    return jax.shard_map(
        shards,
        mesh=mesh,
        in_specs=placed,
        out_specs=(P("bias", "gx", "gy", None, None), P("gx", "gy", "bias")),
        check_vma=False,
    )
```

time: 31.2 us -> 29.6 us (0.949)
  the two profiles are of different devices: /device:TPU:24 before, /device:TPU:1 now
where the time goes in v3:
time: 29.6 us; the launch traced here: 29.5 us
  Pallas kernels  27.6 us (93%)
  local copies, waits for them, and re-layouts  1.24 us (4%)
  between operations  0.64 us (2%)
    pallas_call x1, Pallas kernels, shards(): pl.pallas_call(kernel, out_shape=(jax.ShapeDtypeStruct((BLOCKS, RHS, UNK)...  27.6 us
    unnamed x2, local copies, waits for them, and re-layouts  1.24 us

profile of v3, /device:TPU:1, one launch (start us, length us, event | category | flops | bytes accessed | tf_op | source)
XLA Modules:
  0.0 29.5 jit_solution(18222862646351475825)
XLA Ops:
  0.6 27.6 %shard_map.59 = (bf16[6,32,256]{2,1,0:T(8,128)(2,1)S(1)}, f32[3,2,256]{2,1,0:T(2,128)S(1)}) custom-call(bf16[6,32,256]{2,1,0:T(8,128)(2,1)} %bitcast.12, bf16[6,256,256]{2,1,0:T(8,128)(2,1)} %bitcast.11, bf16[24,256,256]{2,1,0:T(8,128)(2,1)} %bitcast.10, f32[3,2,256]{2,1,0:T(2,128)} %bitcast.13), custom_call_target="tpu_custom_call" | custom-call | flops 403000000 | bytes 4200000 | tf_op jit(solution)/shard_map/pallas_call | solution.py:218
  28.2 0.6 %copy.8 = bf16[1,2,3,32,256]{4,3,2,1,0:T(8,128)(2,1)} copy(bf16[1,2,3,32,256]{4,3,2,1,0:T(8,128)(2,1)S(1)} %bitcast.8) | data formatting | bytes 196608
  28.9 0.6 %copy.9 = f32[2,3,256]{2,0,1:T(2,128)} copy(f32[2,3,256]{2,0,1:T(2,128)S(1)} %bitcast.9) | data formatting | bytes 12288

commit v4 on v3

--- a/solution.py
+++ b/solution.py
@@ -22,8 +22,8 @@
 
 
 def kernel(src_h, inv_h, cp_h, sen_h, adj_out, dop_out,
-           src, inv, cp, sen, a, acc, zs, zr, cs, cr, ys, yr, fold, wz, wy, wr, gs, gr,
-           lsem, ssem, zsem, csem, ysem, wsem, gsem):
+           src, inv, cp, sen, a, acc, zs, zr, cs, cr, ys, yr, both, fold, wz, wy, wr, gs, gr,
+           lsem, ssem, zsem, csem, ysem, wsem, gsem, rsem):
     bias, gx, gy = lax.axis_index("bias"), lax.axis_index("gx"), lax.axis_index("gy")
     nb, nx, ny = lax.axis_size("bias"), lax.axis_size("gx"), lax.axis_size("gy")
     odd = lax.rem(gx, 2)
@@ -35,6 +35,15 @@
     has_y = (gy > 0, gy < ny - 1)
     peers = [lax.rem(bias + step, nb) for step in range(PEERS)]
 
+    ring = nb // 2
+    place, half = lax.rem(bias, ring), bias - lax.rem(bias, ring)
+    round_devs = ({"bias": half + lax.rem(place + 1, ring)}, {"bias": half + lax.rem(place + ring - 1, ring)},
+                  {"bias": lax.rem(bias + ring, nb)})
+
+    def tell(number):
+        for dev in round_devs:
+            pl.semaphore_signal(rsem.at[number], inc=1, device_id=dev, device_id_type=MESH)
+
     def load(from_ref, to_ref, sem):
         pltpu.make_async_copy(from_ref, to_ref, lsem.at[sem]).start()
 
@@ -57,8 +66,8 @@
         pl.semaphore_signal(barrier, inc=1, device_id=dev, device_id_type=MESH)
     for j in range(BY):
         load_tile(4 * (far + j) + 1 - odd, 2)
-    for peer in peers[1:]:
-        pl.semaphore_signal(barrier, inc=1, device_id={"bias": peer}, device_id_type=MESH)
+    for dev in round_devs:
+        pl.semaphore_signal(barrier, inc=1, device_id=dev, device_id_type=MESH)
     load(inv_h.at[near_rows], inv.at[near_rows], 3)
     edge_y = [(i * BY + side * (BY - 1), 3 - side) for side in range(2) for i in range(BX)]
     for k, d in edge_y:
@@ -81,12 +90,13 @@
     for t in range(ITERS):
         if t == 0:
             whole(cp.at[pl.ds(0, BY)], lsem.at[2]).wait()
-        for j in range(BY):
-            zs[t, j] = product(far + j, 1 - odd)
-        if t == 0:
-            pl.semaphore_wait(barrier, 3 + PEERS)
-        for j in range(BY):
-            send(zs.at[t, j], zr.at[t, j], 0, zsem.at[t, j], zdev)
+        if t == 0:
+            for j in range(BY):
+                zs[0, j] = product(far + j, 1 - odd)
+            pl.semaphore_wait(barrier, 4 + 3)
+            for j in range(BY):
+                send(zs.at[0, j], zr.at[0, j], 0, zsem.at[0, j], zdev)
+            tell(0)
         if t == 0:
             for k, d in inner:
                 load_tile(4 * k + d, 7)
@@ -98,29 +108,41 @@
             for i in range(BX):
                 k, d = edge_y[side * BX + i]
                 ys[t, side, i] = product(k, d)
-        for side in range(2):
-            send(ys.at[t, side], yr.at[t, 1 - side], 1, ysem.at[t, 1 - side], ydev[side])
-        if t == 0:
+        if t < ITERS - 1:
+            for side in range(2):
+                send(ys.at[t, side], yr.at[t, 1 - side], 1, ysem.at[t, 1 - side], ydev[side])
+        if t == 0:
+            whole(sen, lsem.at[6]).wait()
+            for k in range(BLOCKS):
+                i, j = divmod(k, BY)
+                h = inv[k].astype(jnp.float32) * sen[j, i:i + 1, :]
+                h = h[:, :128] + h[:, 128:]
+                fold[k] = h + pltpu.roll(h, 64, 1)
+            wz[:UNK] = jnp.where(lane_w, fold[far], fold[far + 1]).astype(jnp.bfloat16)
+            wz[UNK:] = jnp.where(lane_w[:128], fold[far + 2, :128], fold[far + 2, 128:]).astype(jnp.bfloat16)
+            send(wz, wr.at[pl.ds(0, UNK + 128)], 4, wsem, zdev)
+            for j in (0, 2, 1):
+                wy[j] = jnp.where(lane_w, fold[j], fold[BY + j]).astype(jnp.bfloat16)
+            for side in range(2):
+                send(wy.at[side * (BY - 1)], wr.at[pl.ds(UNK + 128 + UNK * (1 - side), UNK)], 4, wsem, ydev[side])
             whole(cp.at[pl.ds(0, BY)], lsem.at[5]).wait()
         for j in range(BY):
             cs[t, j] = product(near + j, odd)
         send(cs.at[t], cr.at[t], 2, csem.at[t], cdev)
         if t == ITERS - 1:
-            whole(wr, wsem).wait()
-            parts = [jnp.where(lane_e, mm(zs[t, 0], wr[0]), mm(zs[t, 1], wr[0])), mm(zs[t, 2], wr[1])]
-            for m, part in enumerate(parts):
-                for p in range(PEERS):
-                    gs[p, m] = part[4 * p:4 * p + 4]
-            for step in range(PEERS - 1, -1, -1):
-                send(gs.at[peers[step], pl.ds(0, 2)], gr.at[pl.ds(2 * step, 2)], 3, gsem, {"bias": peers[step], **zdev})
             for side in range(2):
-                part = jnp.where(lane_e, mm(ys[t, side, 0], wr[2 + side]), mm(ys[t, side, 1], wr[2 + side]))
+                edge = wr[UNK + 128 + UNK * side:2 * UNK + 128 + UNK * side]
+                part = jnp.where(lane_e, mm(ys[t, side, 0], edge), mm(ys[t, side, 1], edge))
                 for p in range(PEERS):
                     gs[p, 2 + side] = part[4 * p:4 * p + 4]
-            for side in range(2):
-                for step in range(PEERS - 1, -1, -1):
+            for step in (6, 2, 5, 7, 1, 3, 4, 0):
+                for side in range(2):
                     send(gs.at[peers[step], pl.ds(2 + side, 1)], gr.at[pl.ds(16 + 8 * (1 - side) + step, 1)], 3, gsem,
                          {"bias": peers[step], **ydev[side]})
+            for j in range(BY):
+                send(zs.at[t, j], zr.at[t, j], 0, zsem.at[t, j], zdev)
+            for side in range(2):
+                send(ys.at[t, side], yr.at[t, 1 - side], 1, ysem.at[t, 1 - side], ydev[side])
         if t == 0:
             whole(cp.at[pl.ds(0, len(inner))], lsem.at[7]).wait()
         for k in range(BLOCKS):
@@ -136,20 +158,10 @@
                 total = total - mm(a[k + 1], cp[4 * (k + 1) + 3])
             acc[k] = total
         if t == 0:
-            whole(sen, lsem.at[6]).wait()
-            for k in range(BLOCKS):
-                i, j = divmod(k, BY)
-                h = inv[k].astype(jnp.float32) * sen[j, i:i + 1, :]
-                h = h[:, :128] + h[:, 128:]
-                fold[k] = h + pltpu.roll(h, 64, 1)
-            for j in range(BY):
-                wy[j] = jnp.where(lane_w, fold[j], fold[BY + j]).astype(jnp.bfloat16)
-            wz[0] = jnp.where(lane_w, fold[far], fold[far + 1]).astype(jnp.bfloat16)
-            wz[1] = fold[far + 2].astype(jnp.bfloat16)
-            for side in range(2):
-                send(wy.at[side * (BY - 1)], wr.at[3 - side], 4, wsem, ydev[side])
-        if t < ITERS - 1:
-            send(wz.at[t], wr.at[t], 4, wsem, zdev)
+            for j in range(BY):
+                both[j] = mm(inv[far + j], cp[4 * (far + j) + 1 - odd]).astype(jnp.bfloat16)
+            pl.semaphore_wait(rsem.at[0], 3)
+            tell(1)
         whole(cr.at[t], csem.at[t]).wait()
         for j in range(BY):
             acc[near + j] = acc[near + j] - cr[t, j].astype(jnp.float32)
@@ -174,9 +186,31 @@
             far_u[j] = far_u[j] - jnp.where(has_y[side], yr[t, side, odd].astype(jnp.float32), 0.0)
         for j in range(BY):
             whole(zr.at[t, j], zsem.at[t, j]).wait()
+        late = []
         for j in range(BY):
             u = far_u[j] - jnp.where(has_z, zr[t, j].astype(jnp.float32), 0.0)
-            a[far + j] = mm(u.astype(jnp.bfloat16), inv[far + j]).astype(jnp.bfloat16)
+            late.append(u.astype(jnp.bfloat16))
+        if t < ITERS - 1:
+            for j in range(BY):
+                zs[t + 1, j] = mm(late[j], both[j]).astype(jnp.bfloat16)
+            if t == 0:
+                pl.semaphore_wait(rsem.at[1], 3)
+            if t + 1 < ITERS - 1:
+                for j in range(BY):
+                    send(zs.at[t + 1, j], zr.at[t + 1, j], 0, zsem.at[t + 1, j], zdev)
+            else:
+                whole(wr, wsem).wait()
+                edge = wr[:UNK]
+                tail = wr[UNK:UNK + 128]
+                parts = [jnp.where(lane_e, mm(zs[t + 1, 0], edge), mm(zs[t + 1, 1], edge)),
+                         mm(zs[t + 1, 2, :, :128], tail) + pltpu.roll(mm(zs[t + 1, 2, :, 128:], tail), 64, 1)]
+                for m, part in enumerate(parts):
+                    for p in range(PEERS):
+                        gs[p, m] = part[4 * p:4 * p + 4]
+                for step in (6, 2, 5, 7, 1, 3, 4, 0):
+                    send(gs.at[peers[step], pl.ds(0, 2)], gr.at[pl.ds(2 * step, 2)], 3, gsem, {"bias": peers[step], **zdev})
+        for j in range(BY):
+            a[far + j] = mm(late[j], inv[far + j]).astype(jnp.bfloat16)
 
     adj_out[...] = a[...]
     whole(zs, ssem.at[0]).wait()
@@ -199,7 +233,8 @@
         pair, last = pair + gr[2 * step], last + gr[2 * step + 1]
     turned = pltpu.roll(pair, 64, 1)
     half = lax.broadcasted_iota(jnp.int32, (4, 128), 1) // 64 == jnp.where(has_z, odd, -1)
-    for j, part in enumerate((jnp.where(lane_g, pair, turned), jnp.where(lane_g, turned, pair), last)):
+    for j, part in enumerate((jnp.where(lane_g, pair, turned), jnp.where(lane_g, turned, pair),
+                              jnp.where(lane_g, last, pltpu.roll(last, 64, 1)))):
         here = totals[j] - jnp.where(half, part, 0.0)
         other = pltpu.roll(here, 64, 1)
         for q in range(0, 4, 2):
@@ -234,13 +269,14 @@
             pltpu.VMEM((ITERS, BY, RHS, UNK), jnp.bfloat16),
             pltpu.VMEM((ITERS, 2, BX, RHS, UNK), jnp.bfloat16),
             pltpu.VMEM((ITERS, 2, BX, RHS, UNK), jnp.bfloat16),
+            pltpu.VMEM((BY, UNK, UNK), jnp.bfloat16),
             pltpu.VMEM((BLOCKS, UNK, 128), jnp.float32),
-            pltpu.VMEM((2, UNK, 128), jnp.bfloat16),
+            pltpu.VMEM((UNK + 128, 128), jnp.bfloat16),
             pltpu.VMEM((BY, UNK, 128), jnp.bfloat16),
-            pltpu.VMEM((4, UNK, 128), jnp.bfloat16),
+            pltpu.VMEM((3 * UNK + 128, 128), jnp.bfloat16),
             pltpu.VMEM((PEERS, 7, 4, 128), jnp.float32),
             pltpu.VMEM((16 + 16 + 3 * (PEERS - 1), 4, 128), jnp.float32),
-            dma((8,)), dma((5,)), dma((ITERS, BY)), dma((ITERS,)), dma((ITERS, 2)), dma(()), dma(()),
+            dma((8,)), dma((5,)), dma((ITERS, BY)), dma((ITERS,)), dma((ITERS, 2)), dma(()), dma(()), pltpu.SemaphoreType.REGULAR((2,)),
         ],
         compiler_params=pltpu.CompilerParams(
             collective_id=0, has_side_effects=True, vmem_limit_bytes=40 * 1024 * 1024),

time: 29.6 us -> 30.8 us (1.041)
  Pallas kernels: 27.6 us -> 28.7 us
    pallas_call x1, Pallas kernels: 27.6 us -> 28.7 us  [shards(): pl.pallas_call(kernel, out_shape=(jax.ShapeDtypeStruct((BLOCKS, RHS, UNK)...]
where the time goes in v4:
time: 30.8 us; the launch traced here: 30.6 us
  Pallas kernels  28.7 us (93%)
  local copies, waits for them, and re-layouts  1.24 us (4%)
  between operations  0.64 us (2%)
    pallas_call x1, Pallas kernels, shards(): pl.pallas_call(kernel, out_shape=(jax.ShapeDtypeStruct((BLOCKS, RHS, UNK)...  28.7 us
    unnamed x2, local copies, waits for them, and re-layouts  1.24 us

profile of v4, /device:TPU:1, one launch (start us, length us, event | category | flops | bytes accessed | tf_op | source)
XLA Modules:
  0.0 30.6 jit_solution(12810541138372964203)
XLA Ops:
  0.6 28.7 %shard_map.59 = (bf16[6,32,256]{2,1,0:T(8,128)(2,1)S(1)}, f32[3,2,256]{2,1,0:T(2,128)S(1)}) custom-call(bf16[6,32,256]{2,1,0:T(8,128)(2,1)} %bitcast.12, bf16[6,256,256]{2,1,0:T(8,128)(2,1)} %bitcast.11, bf16[24,256,256]{2,1,0:T(8,128)(2,1)} %bitcast.10, f32[3,2,256]{2,1,0:T(2,128)} %bitcast.13), custom_call_target="tpu_custom_call" | custom-call | flops 403000000 | bytes 4200000 | tf_op jit(solution)/shard_map/pallas_call | solution.py:253
  29.4 0.6 %copy.8 = bf16[1,2,3,32,256]{4,3,2,1,0:T(8,128)(2,1)} copy(bf16[1,2,3,32,256]{4,3,2,1,0:T(8,128)(2,1)S(1)} %bitcast.8) | data formatting | bytes 196608
  30.0 0.6 %copy.9 = f32[2,3,256]{2,0,1:T(2,128)} copy(f32[2,3,256]{2,0,1:T(2,128)S(1)} %bitcast.9) | data formatting | bytes 12288

commit v5 on v4

--- a/solution.py
+++ b/solution.py
@@ -94,8 +94,7 @@
             for j in range(BY):
                 zs[0, j] = product(far + j, 1 - odd)
             pl.semaphore_wait(barrier, 4 + 3)
-            for j in range(BY):
-                send(zs.at[0, j], zr.at[0, j], 0, zsem.at[0, j], zdev)
+            send(zs.at[0], zr.at[0], 0, zsem.at[0], zdev)
             tell(0)
         if t == 0:
             for k, d in inner:
@@ -110,7 +109,7 @@
                 ys[t, side, i] = product(k, d)
         if t < ITERS - 1:
             for side in range(2):
-                send(ys.at[t, side], yr.at[t, 1 - side], 1, ysem.at[t, 1 - side], ydev[side])
+                send(ys.at[t, side], yr.at[t, 1 - side], 1, ysem.at[t], ydev[side])
         if t == 0:
             whole(sen, lsem.at[6]).wait()
             for k in range(BLOCKS):
@@ -139,10 +138,9 @@
                 for side in range(2):
                     send(gs.at[peers[step], pl.ds(2 + side, 1)], gr.at[pl.ds(16 + 8 * (1 - side) + step, 1)], 3, gsem,
                          {"bias": peers[step], **ydev[side]})
-            for j in range(BY):
-                send(zs.at[t, j], zr.at[t, j], 0, zsem.at[t, j], zdev)
+            send(zs.at[t], zr.at[t], 0, zsem.at[t], zdev)
             for side in range(2):
-                send(ys.at[t, side], yr.at[t, 1 - side], 1, ysem.at[t, 1 - side], ydev[side])
+                send(ys.at[t, side], yr.at[t, 1 - side], 1, ysem.at[t], ydev[side])
         if t == 0:
             whole(cp.at[pl.ds(0, len(inner))], lsem.at[7]).wait()
         for k in range(BLOCKS):
@@ -174,8 +172,7 @@
                 send(gs.at[peers[step], pl.ds(4, 3)], gr.at[pl.ds(32 + 3 * (step - 1), 3)], 3, gsem, {"bias": peers[step]})
         near_u = [acc[near + j] for j in range(BY)]
         a[near + 1] = mm(near_u[1].astype(jnp.bfloat16), inv[near + 1]).astype(jnp.bfloat16)
-        for side in range(2):
-            whole(yr.at[t, side], ysem.at[t, side]).wait()
+        whole(yr.at[t], ysem.at[t]).wait()
         for side in range(2):
             j = side * (BY - 1)
             u = near_u[j] - jnp.where(has_y[side], yr[t, side, 1 - odd].astype(jnp.float32), 0.0)
@@ -184,8 +181,7 @@
         for side in range(2):
             j = side * (BY - 1)
             far_u[j] = far_u[j] - jnp.where(has_y[side], yr[t, side, odd].astype(jnp.float32), 0.0)
-        for j in range(BY):
-            whole(zr.at[t, j], zsem.at[t, j]).wait()
+        whole(zr.at[t], zsem.at[t]).wait()
         late = []
         for j in range(BY):
             u = far_u[j] - jnp.where(has_z, zr[t, j].astype(jnp.float32), 0.0)
@@ -196,8 +192,7 @@
             if t == 0:
                 pl.semaphore_wait(rsem.at[1], 3)
             if t + 1 < ITERS - 1:
-                for j in range(BY):
-                    send(zs.at[t + 1, j], zr.at[t + 1, j], 0, zsem.at[t + 1, j], zdev)
+                send(zs.at[t + 1], zr.at[t + 1], 0, zsem.at[t + 1], zdev)
             else:
                 whole(wr, wsem).wait()
                 edge = wr[:UNK]
@@ -241,6 +236,15 @@
             dop_out[j, 0:1, 64 * q:64 * q + 128] = jnp.where(lane_g[:1], here[q:q + 1], other[q + 1:q + 2])
             dop_out[j, 1:2, 64 * q:64 * q + 128] = jnp.where(lane_g[:1], other[q:q + 1], here[q + 1:q + 2])
     whole(gr, ssem.at[3]).wait()
+
+
+def finish(adj_in, dop_in, adj_out, dop_out, sem):
+    first = pltpu.make_async_copy(adj_in, adj_out, sem.at[0])
+    second = pltpu.make_async_copy(dop_in, dop_out, sem.at[1])
+    first.start()
+    second.start()
+    first.wait()
+    second.wait()
 
 
 def shards(source, inverse, coupling, sensitivity):
@@ -276,12 +280,21 @@
             pltpu.VMEM((3 * UNK + 128, 128), jnp.bfloat16),
             pltpu.VMEM((PEERS, 7, 4, 128), jnp.float32),
             pltpu.VMEM((16 + 16 + 3 * (PEERS - 1), 4, 128), jnp.float32),
-            dma((8,)), dma((5,)), dma((ITERS, BY)), dma((ITERS,)), dma((ITERS, 2)), dma(()), dma(()), pltpu.SemaphoreType.REGULAR((2,)),
+            dma((8,)), dma((5,)), dma((ITERS,)), dma((ITERS,)), dma((ITERS,)), dma(()), dma(()), pltpu.SemaphoreType.REGULAR((2,)),
         ],
         compiler_params=pltpu.CompilerParams(
             collective_id=0, has_side_effects=True, vmem_limit_bytes=40 * 1024 * 1024),
         cost_estimate=pl.CostEstimate(flops=403_000_000, bytes_accessed=4_200_000, transcendentals=0),
     )(*(pltpu.with_memory_space_constraint(x, pltpu.HBM) for x in (src, inv, cp, sen)))
+    adjoint, doping = pl.pallas_call(
+        finish,
+        out_shape=(jax.ShapeDtypeStruct((BLOCKS, RHS, UNK), jnp.bfloat16),
+                   jax.ShapeDtypeStruct((BY, BX, UNK), jnp.float32)),
+        in_specs=[pl.BlockSpec(memory_space=pltpu.VMEM)] * 2,
+        out_specs=(pl.BlockSpec(memory_space=pl.ANY),) * 2,
+        scratch_shapes=[dma((2,))],
+        compiler_params=pltpu.CompilerParams(vmem_limit_bytes=40 * 1024 * 1024),
+    )(adjoint, doping)
     return (adjoint.reshape(1, BX, BY, RHS, UNK), doping.transpose(1, 0, 2))
 
 

time: 30.8 us -> 30.1 us (0.977)
  local copies, waits for them, and re-layouts: 1.24 us -> 0 us
  Pallas kernels: 28.7 us -> 29.3 us
    unnamed x2 -> x0, local copies, waits for them, and re-layouts: 1.24 us -> none
    pallas_call x0 -> x1, Pallas kernels: none -> 0.66 us  [shards(): pl.pallas_call(finish, out_shape=(jax.ShapeDtypeStruct((BLOCKS, RHS, UNK)...]
where the time goes in v5:
time: 30.1 us; the launch traced here: 29.9 us
  Pallas kernels  29.3 us (97%)
  between operations  0.64 us (2%)
    pallas_call x1, Pallas kernels, shards(): pl.pallas_call(kernel, out_shape=(jax.ShapeDtypeStruct((BLOCKS, RHS, UNK)...  28.6 us
    pallas_call x1, Pallas kernels, shards(): pl.pallas_call(finish, out_shape=(jax.ShapeDtypeStruct((BLOCKS, RHS, UNK)...  0.66 us

profile of v5, /device:TPU:1, one launch (start us, length us, event | category | flops | bytes accessed | tf_op | source)
XLA Modules:
  0.0 29.9 jit_solution(3909614848686707839)
XLA Ops:
  0.6 28.6 %shard_map.59 = (bf16[6,32,256]{2,1,0:T(8,128)(2,1)S(1)}, f32[3,2,256]{2,1,0:T(2,128)S(1)}) custom-call(bf16[6,32,256]{2,1,0:T(8,128)(2,1)} %bitcast.10, bf16[6,256,256]{2,1,0:T(8,128)(2,1)} %bitcast.9, bf16[24,256,256]{2,1,0:T(8,128)(2,1)} %bitcast.8, f32[3,2,256]{2,1,0:T(2,128)} %bitcast.11), custom_call_target="tpu_custom_call" | custom-call | flops 403000000 | bytes 4200000 | tf_op jit(solution)/shard_map/pallas_call | solution.py:257
  29.3 0.7 %shard_map.60 = (bf16[6,32,256]{2,1,0:T(8,128)(2,1)}, f32[3,2,256]{2,1,0:T(2,128)}) custom-call(bf16[6,32,256]{2,1,0:T(8,128)(2,1)S(1)} %get-tuple-element.6.adj_in, f32[3,2,256]{2,1,0:T(2,128)S(1)} %get-tuple-element.7.dop_in), custom_call_target="tpu_custom_call" | custom-call | tf_op jit(solution)/shard_map/pallas_call | solution.py:289

commit v6 on v5

--- a/solution.py
+++ b/solution.py
@@ -58,12 +58,33 @@
             src_ref=from_ref, dst_ref=to_ref, send_sem=ssem.at[sent], recv_sem=landed,
             device_id=dev, device_id_type=MESH).start()
 
+    def send_z(t):
+        @pl.when(has_z)
+        def _():
+            send(zs.at[t], zr.at[t], 0, zsem.at[t], zdev)
+
+    def send_y(t):
+        for side in range(2):
+            @pl.when(has_y[side])
+            def _():
+                send(ys.at[side, t], yr.at[1 - side, t], 3 + side, ysem.at[1 - side, t], ydev[side])
+
+    def wait_if(there, *pairs):
+        @pl.when(there)
+        def _():
+            for ref, sem in pairs:
+                whole(ref, sem).wait()
+
     far_rows, near_rows = pl.ds(far, BY), pl.ds(near, BY)
     load(src_h, src, 0)
     load(inv_h.at[far_rows], inv.at[far_rows], 1)
     barrier = pltpu.get_barrier_semaphore()
-    for dev in (zdev,) + ydev + (cdev,):
-        pl.semaphore_signal(barrier, inc=1, device_id=dev, device_id_type=MESH)
+    for dev, there in ((zdev, has_z), (ydev[0], has_y[0]), (ydev[1], has_y[1])):
+        @pl.when(there)
+        def _():
+            pl.semaphore_signal(barrier, inc=1, device_id=dev, device_id_type=MESH)
+    pl.semaphore_signal(barrier, inc=1, device_id=cdev, device_id_type=MESH)
+    greeted = 4 + sum(there.astype(jnp.int32) for there in (has_z,) + has_y)
     for j in range(BY):
         load_tile(4 * (far + j) + 1 - odd, 2)
     for dev in round_devs:
@@ -76,6 +97,19 @@
         load_tile(4 * (near + j) + odd, 5)
     load(sen_h, sen, 6)
 
+    @pl.when(jnp.logical_not(has_z))
+    def _():
+        zr[...] = jnp.zeros_like(zr)
+        wr[:UNK + 128] = jnp.zeros((UNK + 128, 128), jnp.bfloat16)
+        gr[:16] = jnp.zeros((16, 4, 128), jnp.float32)
+
+    for side in range(2):
+        @pl.when(jnp.logical_not(has_y[side]))
+        def _():
+            yr[side] = jnp.zeros((ITERS, BX, RHS, UNK), jnp.bfloat16)
+            wr[UNK + 128 + UNK * side:2 * UNK + 128 + UNK * side] = jnp.zeros((UNK, 128), jnp.bfloat16)
+            gr[16 + 8 * side:24 + 8 * side] = jnp.zeros((8, 4, 128), jnp.float32)
+
     whole(src, lsem.at[0]).wait()
     whole(inv.at[far_rows], lsem.at[1]).wait()
     for j in range(BY):
@@ -93,8 +127,8 @@
         if t == 0:
             for j in range(BY):
                 zs[0, j] = product(far + j, 1 - odd)
-            pl.semaphore_wait(barrier, 4 + 3)
-            send(zs.at[0], zr.at[0], 0, zsem.at[0], zdev)
+            pl.semaphore_wait(barrier, greeted)
+            send_z(0)
             tell(0)
         if t == 0:
             for k, d in inner:
@@ -106,10 +140,9 @@
         for side in range(2):
             for i in range(BX):
                 k, d = edge_y[side * BX + i]
-                ys[t, side, i] = product(k, d)
+                ys[side, t, i] = product(k, d)
         if t < ITERS - 1:
-            for side in range(2):
-                send(ys.at[t, side], yr.at[t, 1 - side], 1, ysem.at[t], ydev[side])
+            send_y(t)
         if t == 0:
             whole(sen, lsem.at[6]).wait()
             for k in range(BLOCKS):
@@ -119,28 +152,37 @@
                 fold[k] = h + pltpu.roll(h, 64, 1)
             wz[:UNK] = jnp.where(lane_w, fold[far], fold[far + 1]).astype(jnp.bfloat16)
             wz[UNK:] = jnp.where(lane_w[:128], fold[far + 2, :128], fold[far + 2, 128:]).astype(jnp.bfloat16)
-            send(wz, wr.at[pl.ds(0, UNK + 128)], 4, wsem, zdev)
+
+            @pl.when(has_z)
+            def _():
+                send(wz, wr.at[pl.ds(0, UNK + 128)], 1, wsem.at[0], zdev)
+
             for j in (0, 2, 1):
                 wy[j] = jnp.where(lane_w, fold[j], fold[BY + j]).astype(jnp.bfloat16)
             for side in range(2):
-                send(wy.at[side * (BY - 1)], wr.at[pl.ds(UNK + 128 + UNK * (1 - side), UNK)], 4, wsem, ydev[side])
+                @pl.when(has_y[side])
+                def _():
+                    send(wy.at[side * (BY - 1)], wr.at[pl.ds(UNK + 128 + UNK * (1 - side), UNK)], 5 + side, wsem.at[2 - side], ydev[side])
             whole(cp.at[pl.ds(0, BY)], lsem.at[5]).wait()
         for j in range(BY):
             cs[t, j] = product(near + j, odd)
-        send(cs.at[t], cr.at[t], 2, csem.at[t], cdev)
+        send(cs.at[t], cr.at[t], 9, csem.at[t], cdev)
         if t == ITERS - 1:
             for side in range(2):
+                wait_if(has_y[side], (wr.at[pl.ds(UNK + 128 + UNK * side, UNK)], wsem.at[1 + side]))
                 edge = wr[UNK + 128 + UNK * side:2 * UNK + 128 + UNK * side]
-                part = jnp.where(lane_e, mm(ys[t, side, 0], edge), mm(ys[t, side, 1], edge))
+                part = jnp.where(lane_e, mm(ys[side, t, 0], edge), mm(ys[side, t, 1], edge))
                 for p in range(PEERS):
                     gs[p, 2 + side] = part[4 * p:4 * p + 4]
-            for step in (6, 2, 5, 7, 1, 3, 4, 0):
-                for side in range(2):
-                    send(gs.at[peers[step], pl.ds(2 + side, 1)], gr.at[pl.ds(16 + 8 * (1 - side) + step, 1)], 3, gsem,
-                         {"bias": peers[step], **ydev[side]})
-            send(zs.at[t], zr.at[t], 0, zsem.at[t], zdev)
             for side in range(2):
-                send(ys.at[t, side], yr.at[t, 1 - side], 1, ysem.at[t], ydev[side])
+                @pl.when(has_y[side])
+                def _():
+                    for step in (6, 2, 5, 7, 1, 3, 4, 0):
+                        send(gs.at[peers[step], pl.ds(2 + side, 1)], gr.at[pl.ds(16 + 8 * (1 - side) + step, 1)], 7 + side,
+                             gsem.at[3 - side], {"bias": peers[step], **ydev[side]})
+
+            send_z(t)
+            send_y(t)
         if t == 0:
             whole(cp.at[pl.ds(0, len(inner))], lsem.at[7]).wait()
         for k in range(BLOCKS):
@@ -169,19 +211,20 @@
                 for p in range(PEERS):
                     gs[p, 4 + j] = part[4 * p:4 * p + 4]
             for step in (6, 2, 5, 7, 1, 3, 4):
-                send(gs.at[peers[step], pl.ds(4, 3)], gr.at[pl.ds(32 + 3 * (step - 1), 3)], 3, gsem, {"bias": peers[step]})
+                send(gs.at[peers[step], pl.ds(4, 3)], gr.at[pl.ds(32 + 3 * (step - 1), 3)], 10, gsem.at[0], {"bias": peers[step]})
         near_u = [acc[near + j] for j in range(BY)]
         a[near + 1] = mm(near_u[1].astype(jnp.bfloat16), inv[near + 1]).astype(jnp.bfloat16)
-        whole(yr.at[t], ysem.at[t]).wait()
+        for side in range(2):
+            wait_if(has_y[side], (yr.at[side, t], ysem.at[side, t]))
         for side in range(2):
             j = side * (BY - 1)
-            u = near_u[j] - jnp.where(has_y[side], yr[t, side, 1 - odd].astype(jnp.float32), 0.0)
+            u = near_u[j] - jnp.where(has_y[side], yr[side, t, 1 - odd].astype(jnp.float32), 0.0)
             a[near + j] = mm(u.astype(jnp.bfloat16), inv[near + j]).astype(jnp.bfloat16)
         far_u = [acc[far + j] for j in range(BY)]
         for side in range(2):
             j = side * (BY - 1)
-            far_u[j] = far_u[j] - jnp.where(has_y[side], yr[t, side, odd].astype(jnp.float32), 0.0)
-        whole(zr.at[t], zsem.at[t]).wait()
+            far_u[j] = far_u[j] - jnp.where(has_y[side], yr[side, t, odd].astype(jnp.float32), 0.0)
+        wait_if(has_z, (zr.at[t], zsem.at[t]))
         late = []
         for j in range(BY):
             u = far_u[j] - jnp.where(has_z, zr[t, j].astype(jnp.float32), 0.0)
@@ -192,9 +235,9 @@
             if t == 0:
                 pl.semaphore_wait(rsem.at[1], 3)
             if t + 1 < ITERS - 1:
-                send(zs.at[t + 1], zr.at[t + 1], 0, zsem.at[t + 1], zdev)
+                send_z(t + 1)
             else:
-                whole(wr, wsem).wait()
+                wait_if(has_z, (wr.at[pl.ds(0, UNK + 128)], wsem.at[0]))
                 edge = wr[:UNK]
                 tail = wr[UNK:UNK + 128]
                 parts = [jnp.where(lane_e, mm(zs[t + 1, 0], edge), mm(zs[t + 1, 1], edge)),
@@ -202,18 +245,22 @@
                 for m, part in enumerate(parts):
                     for p in range(PEERS):
                         gs[p, m] = part[4 * p:4 * p + 4]
-                for step in (6, 2, 5, 7, 1, 3, 4, 0):
-                    send(gs.at[peers[step], pl.ds(0, 2)], gr.at[pl.ds(2 * step, 2)], 3, gsem, {"bias": peers[step], **zdev})
+
+                @pl.when(has_z)
+                def _():
+                    for step in (6, 2, 5, 7, 1, 3, 4, 0):
+                        send(gs.at[peers[step], pl.ds(0, 2)], gr.at[pl.ds(2 * step, 2)], 2, gsem.at[1], {"bias": peers[step], **zdev})
+
         for j in range(BY):
             a[far + j] = mm(late[j], inv[far + j]).astype(jnp.bfloat16)
 
     adj_out[...] = a[...]
-    whole(zs, ssem.at[0]).wait()
-    whole(ys, ssem.at[1]).wait()
-    whole(cs, ssem.at[2]).wait()
-    whole(wr, ssem.at[4]).wait()
+    whole(cs, ssem.at[9]).wait()
     totals = [gs[bias, 4 + j] for j in range(BY)]
-    whole(gr, gsem).wait()
+    whole(gr.at[pl.ds(32, 3 * (PEERS - 1))], gsem.at[0]).wait()
+    wait_if(has_z, (gr.at[pl.ds(0, 16)], gsem.at[1]))
+    for side in range(2):
+        wait_if(has_y[side], (gr.at[pl.ds(16 + 8 * side, 8)], gsem.at[2 + side]))
     for step in range(1, PEERS):
         for j in range(BY):
             totals[j] = totals[j] + gr[32 + 3 * (step - 1) + j]
@@ -235,7 +282,11 @@
         for q in range(0, 4, 2):
             dop_out[j, 0:1, 64 * q:64 * q + 128] = jnp.where(lane_g[:1], here[q:q + 1], other[q + 1:q + 2])
             dop_out[j, 1:2, 64 * q:64 * q + 128] = jnp.where(lane_g[:1], other[q:q + 1], here[q + 1:q + 2])
-    whole(gr, ssem.at[3]).wait()
+    whole(gr.at[pl.ds(32, 3 * (PEERS - 1))], ssem.at[10]).wait()
+    wait_if(has_z, (zs, ssem.at[0]), (wz, ssem.at[1]), (gr.at[pl.ds(0, 16)], ssem.at[2]))
+    for side in range(2):
+        wait_if(has_y[side], (ys.at[side], ssem.at[3 + side]), (wy.at[0], ssem.at[5 + side]),
+                (gr.at[pl.ds(16, 8)], ssem.at[7 + side]))
 
 
 def finish(adj_in, dop_in, adj_out, dop_out, sem):
@@ -271,8 +322,8 @@
             pltpu.VMEM((ITERS, BY, RHS, UNK), jnp.bfloat16),
             pltpu.VMEM((ITERS, BY, RHS, UNK), jnp.bfloat16),
             pltpu.VMEM((ITERS, BY, RHS, UNK), jnp.bfloat16),
-            pltpu.VMEM((ITERS, 2, BX, RHS, UNK), jnp.bfloat16),
-            pltpu.VMEM((ITERS, 2, BX, RHS, UNK), jnp.bfloat16),
+            pltpu.VMEM((2, ITERS, BX, RHS, UNK), jnp.bfloat16),
+            pltpu.VMEM((2, ITERS, BX, RHS, UNK), jnp.bfloat16),
             pltpu.VMEM((BY, UNK, UNK), jnp.bfloat16),
             pltpu.VMEM((BLOCKS, UNK, 128), jnp.float32),
             pltpu.VMEM((UNK + 128, 128), jnp.bfloat16),
@@ -280,7 +331,7 @@
             pltpu.VMEM((3 * UNK + 128, 128), jnp.bfloat16),
             pltpu.VMEM((PEERS, 7, 4, 128), jnp.float32),
             pltpu.VMEM((16 + 16 + 3 * (PEERS - 1), 4, 128), jnp.float32),
-            dma((8,)), dma((5,)), dma((ITERS,)), dma((ITERS,)), dma((ITERS,)), dma(()), dma(()), pltpu.SemaphoreType.REGULAR((2,)),
+            dma((8,)), dma((11,)), dma((ITERS,)), dma((ITERS,)), dma((2, ITERS)), dma((3,)), dma((4,)), pltpu.SemaphoreType.REGULAR((2,)),
         ],
         compiler_params=pltpu.CompilerParams(
             collective_id=0, has_side_effects=True, vmem_limit_bytes=40 * 1024 * 1024),

time: 30.1 us -> 26.2 us (0.87)
  the two profiles are of different devices: /device:TPU:1 before, /device:TPU:153 now
where the time goes in v6:
time: 26.2 us; the launch traced here: 26 us
  Pallas kernels  25.4 us (97%)
  between operations  0.64 us (2%)
    pallas_call x1, Pallas kernels, shards(): pl.pallas_call(kernel, out_shape=(jax.ShapeDtypeStruct((BLOCKS, RHS, UNK)...  24.7 us
    pallas_call x1, Pallas kernels, shards(): pl.pallas_call(finish, out_shape=(jax.ShapeDtypeStruct((BLOCKS, RHS, UNK)...  0.66 us

profile of v6, /device:TPU:153, one launch (start us, length us, event | category | flops | bytes accessed | tf_op | source)
XLA Modules:
  0.0 26.0 jit_solution(3557470817685391323)
XLA Ops:
  0.6 24.7 %shard_map.59 = (bf16[6,32,256]{2,1,0:T(8,128)(2,1)S(1)}, f32[3,2,256]{2,1,0:T(2,128)S(1)}) custom-call(bf16[6,32,256]{2,1,0:T(8,128)(2,1)} %bitcast.10, bf16[6,256,256]{2,1,0:T(8,128)(2,1)} %bitcast.9, bf16[24,256,256]{2,1,0:T(8,128)(2,1)} %bitcast.8, f32[3,2,256]{2,1,0:T(2,128)} %bitcast.11), custom_call_target="tpu_custom_call" | custom-call | flops 403000000 | bytes 4200000 | tf_op jit(solution)/shard_map/pallas_call | solution.py:308
  25.4 0.7 %shard_map.60 = (bf16[6,32,256]{2,1,0:T(8,128)(2,1)}, f32[3,2,256]{2,1,0:T(2,128)}) custom-call(bf16[6,32,256]{2,1,0:T(8,128)(2,1)S(1)} %get-tuple-element.6.adj_in, f32[3,2,256]{2,1,0:T(2,128)S(1)} %get-tuple-element.7.dop_in), custom_call_target="tpu_custom_call" | custom-call | tf_op jit(solution)/shard_map/pallas_call | solution.py:340

commit v7 on v6

--- a/solution.py
+++ b/solution.py
@@ -218,16 +218,16 @@
             wait_if(has_y[side], (yr.at[side, t], ysem.at[side, t]))
         for side in range(2):
             j = side * (BY - 1)
-            u = near_u[j] - jnp.where(has_y[side], yr[side, t, 1 - odd].astype(jnp.float32), 0.0)
+            u = near_u[j] - yr[side, t, 1 - odd].astype(jnp.float32)
             a[near + j] = mm(u.astype(jnp.bfloat16), inv[near + j]).astype(jnp.bfloat16)
         far_u = [acc[far + j] for j in range(BY)]
         for side in range(2):
             j = side * (BY - 1)
-            far_u[j] = far_u[j] - jnp.where(has_y[side], yr[side, t, odd].astype(jnp.float32), 0.0)
+            far_u[j] = far_u[j] - yr[side, t, odd].astype(jnp.float32)
         wait_if(has_z, (zr.at[t], zsem.at[t]))
         late = []
         for j in range(BY):
-            u = far_u[j] - jnp.where(has_z, zr[t, j].astype(jnp.float32), 0.0)
+            u = far_u[j] - zr[t, j].astype(jnp.float32)
             late.append(u.astype(jnp.bfloat16))
         if t < ITERS - 1:
             for j in range(BY):
@@ -256,6 +256,11 @@
 
     adj_out[...] = a[...]
     whole(cs, ssem.at[9]).wait()
+    whole(gr.at[pl.ds(32, 3 * (PEERS - 1))], ssem.at[10]).wait()
+    wait_if(has_z, (zs, ssem.at[0]), (wz, ssem.at[1]), (gr.at[pl.ds(0, 16)], ssem.at[2]))
+    for side in range(2):
+        wait_if(has_y[side], (ys.at[side], ssem.at[3 + side]), (wy.at[0], ssem.at[5 + side]),
+                (gr.at[pl.ds(16, 8)], ssem.at[7 + side]))
     totals = [gs[bias, 4 + j] for j in range(BY)]
     whole(gr.at[pl.ds(32, 3 * (PEERS - 1))], gsem.at[0]).wait()
     wait_if(has_z, (gr.at[pl.ds(0, 16)], gsem.at[1]))
@@ -269,12 +274,12 @@
         for step in range(1, PEERS):
             part = part + gr[16 + 8 * side + step]
         j = side * (BY - 1)
-        totals[j] = totals[j] - jnp.where(has_y[side], part, 0.0)
+        totals[j] = totals[j] - part
     pair, last = gr[0], gr[1]
     for step in range(1, PEERS):
         pair, last = pair + gr[2 * step], last + gr[2 * step + 1]
     turned = pltpu.roll(pair, 64, 1)
-    half = lax.broadcasted_iota(jnp.int32, (4, 128), 1) // 64 == jnp.where(has_z, odd, -1)
+    half = lax.broadcasted_iota(jnp.int32, (4, 128), 1) // 64 == odd
     for j, part in enumerate((jnp.where(lane_g, pair, turned), jnp.where(lane_g, turned, pair),
                               jnp.where(lane_g, last, pltpu.roll(last, 64, 1)))):
         here = totals[j] - jnp.where(half, part, 0.0)
@@ -282,11 +287,6 @@
         for q in range(0, 4, 2):
             dop_out[j, 0:1, 64 * q:64 * q + 128] = jnp.where(lane_g[:1], here[q:q + 1], other[q + 1:q + 2])
             dop_out[j, 1:2, 64 * q:64 * q + 128] = jnp.where(lane_g[:1], other[q:q + 1], here[q + 1:q + 2])
-    whole(gr.at[pl.ds(32, 3 * (PEERS - 1))], ssem.at[10]).wait()
-    wait_if(has_z, (zs, ssem.at[0]), (wz, ssem.at[1]), (gr.at[pl.ds(0, 16)], ssem.at[2]))
-    for side in range(2):
-        wait_if(has_y[side], (ys.at[side], ssem.at[3 + side]), (wy.at[0], ssem.at[5 + side]),
-                (gr.at[pl.ds(16, 8)], ssem.at[7 + side]))
 
 
 def finish(adj_in, dop_in, adj_out, dop_out, sem):

time: 26.2 us -> 26.2 us (level)
  no operation moved by 1% of the time
where the time goes in v7:
time: 26.2 us; the launch traced here: 26 us
  Pallas kernels  25.4 us (97%)
  between operations  0.64 us (2%)
    pallas_call x1, Pallas kernels, shards(): pl.pallas_call(kernel, out_shape=(jax.ShapeDtypeStruct((BLOCKS, RHS, UNK)...  24.7 us
    pallas_call x1, Pallas kernels, shards(): pl.pallas_call(finish, out_shape=(jax.ShapeDtypeStruct((BLOCKS, RHS, UNK)...  0.66 us

profile of v7, /device:TPU:153, one launch (start us, length us, event | category | flops | bytes accessed | tf_op | source)
XLA Modules:
  0.0 26.0 jit_solution(5009158250739900850)
XLA Ops:
  0.6 24.7 %shard_map.59 = (bf16[6,32,256]{2,1,0:T(8,128)(2,1)S(1)}, f32[3,2,256]{2,1,0:T(2,128)S(1)}) custom-call(bf16[6,32,256]{2,1,0:T(8,128)(2,1)} %bitcast.10, bf16[6,256,256]{2,1,0:T(8,128)(2,1)} %bitcast.9, bf16[24,256,256]{2,1,0:T(8,128)(2,1)} %bitcast.8, f32[3,2,256]{2,1,0:T(2,128)} %bitcast.11), custom_call_target="tpu_custom_call" | custom-call | flops 403000000 | bytes 4200000 | tf_op jit(solution)/shard_map/pallas_call | solution.py:308
  25.3 0.7 %shard_map.60 = (bf16[6,32,256]{2,1,0:T(8,128)(2,1)}, f32[3,2,256]{2,1,0:T(2,128)}) custom-call(bf16[6,32,256]{2,1,0:T(8,128)(2,1)S(1)} %get-tuple-element.6.adj_in, f32[3,2,256]{2,1,0:T(2,128)S(1)} %get-tuple-element.7.dop_in), custom_call_target="tpu_custom_call" | custom-call | tf_op jit(solution)/shard_map/pallas_call | solution.py:340

commit v8 on v6

--- a/solution.py
+++ b/solution.py
@@ -137,6 +137,10 @@
             for j in range(BY):
                 a[near + j] = mm(src[near + j], inv[near + j]).astype(jnp.bfloat16)
             whole(cp.at[pl.ds(0, 2 * BX)], lsem.at[4]).wait()
+        if t == ITERS - 1:
+            for j in range(BY):
+                cs[t, j] = product(near + j, odd)
+            send(cs.at[t], cr.at[t], 9, csem.at[t], cdev)
         for side in range(2):
             for i in range(BX):
                 k, d = edge_y[side * BX + i]
@@ -164,9 +168,10 @@
                 def _():
                     send(wy.at[side * (BY - 1)], wr.at[pl.ds(UNK + 128 + UNK * (1 - side), UNK)], 5 + side, wsem.at[2 - side], ydev[side])
             whole(cp.at[pl.ds(0, BY)], lsem.at[5]).wait()
-        for j in range(BY):
-            cs[t, j] = product(near + j, odd)
-        send(cs.at[t], cr.at[t], 9, csem.at[t], cdev)
+        if t < ITERS - 1:
+            for j in range(BY):
+                cs[t, j] = product(near + j, odd)
+            send(cs.at[t], cr.at[t], 9, csem.at[t], cdev)
         if t == ITERS - 1:
             for side in range(2):
                 wait_if(has_y[side], (wr.at[pl.ds(UNK + 128 + UNK * side, UNK)], wsem.at[1 + side]))

time: 26.2 us -> 26.1 us (level)
  no operation moved by 1% of the time
where the time goes in v8:
time: 26.1 us; the launch traced here: 25.9 us
  Pallas kernels  25.3 us (97%)
  between operations  0.64 us (2%)
    pallas_call x1, Pallas kernels, shards(): pl.pallas_call(kernel, out_shape=(jax.ShapeDtypeStruct((BLOCKS, RHS, UNK)...  24.6 us
    pallas_call x1, Pallas kernels, shards(): pl.pallas_call(finish, out_shape=(jax.ShapeDtypeStruct((BLOCKS, RHS, UNK)...  0.66 us

profile of v8, /device:TPU:153, one launch (start us, length us, event | category | flops | bytes accessed | tf_op | source)
XLA Modules:
  0.0 25.9 jit_solution(15037163224938277477)
XLA Ops:
  0.6 24.6 %shard_map.59 = (bf16[6,32,256]{2,1,0:T(8,128)(2,1)S(1)}, f32[3,2,256]{2,1,0:T(2,128)S(1)}) custom-call(bf16[6,32,256]{2,1,0:T(8,128)(2,1)} %bitcast.10, bf16[6,256,256]{2,1,0:T(8,128)(2,1)} %bitcast.9, bf16[24,256,256]{2,1,0:T(8,128)(2,1)} %bitcast.8, f32[3,2,256]{2,1,0:T(2,128)} %bitcast.11), custom_call_target="tpu_custom_call" | custom-call | flops 403000000 | bytes 4200000 | tf_op jit(solution)/shard_map/pallas_call | solution.py:313
  25.2 0.7 %shard_map.60 = (bf16[6,32,256]{2,1,0:T(8,128)(2,1)}, f32[3,2,256]{2,1,0:T(2,128)}) custom-call(bf16[6,32,256]{2,1,0:T(8,128)(2,1)S(1)} %get-tuple-element.6.adj_in, f32[3,2,256]{2,1,0:T(2,128)S(1)} %get-tuple-element.7.dop_in), custom_call_target="tpu_custom_call" | custom-call | tf_op jit(solution)/shard_map/pallas_call | solution.py:345
